TPU v7x, 32 devices: a whole 2x2x4 slice. The times are simulated.
32 devices in a mesh: groups: 2 (over y), dp: 4 (over x, core), owner: 4 (over z).
Axes of the slice: x: 2, y: 2, z: 4, core: 2. Of those that a mesh axis runs over, the one named last changes fastest.
Arguments:
- acts: bfloat16 [8192, 6144], P(('groups', 'dp'), 'owner'), parts along dimension 0, may hold values from -45 to 45
- out_grads: bfloat16 [8192, 24576], P(('groups', 'dp'), 'owner'), parts along dimension 0, may hold values from -45 to 45
- weight_grad: bfloat16 [12288, 24576], P(('groups', 'owner'), 'dp'), parts along dimension 0, may hold values from -6 to 6
- old_bases: bfloat16 [8, 4, 16, 256, 256], P(('groups', 'owner'), 'dp'), parts along dimension 0, may hold values from -0.5 to 1.5
- owner_table: int32 [4, 30, 1], P('owner'), may hold values from 0 to 3; in each aligned block of 30 rows (0 to 29, 30 to 59, ..., all dimensions but the last counted through in order) at most 16 rows name the same one
Outputs:
- preconditioned: bfloat16 [12288, 24576], P(('groups', 'owner'), 'dp'), parts along dimension 0
- new_bases: bfloat16 [8, 4, 16, 256, 256], P(('groups', 'owner'), 'dp'), parts along dimension 0
- new_values: bfloat16 [8, 4, 16, 256], P(('groups', 'owner'), 'dp'), parts along dimension 0
There are 2 independent parts, one for each index of `groups`. A program takes and returns all parts, laid end to end along the dimension named above; an argument that names none is the same for every part. Nothing has to cross between parts.
Inputs may be any that keep to these rules, and one draw needn't show every extreme that they name: `owner_table`: within one column's 30 entries a dp index appears at most 16 times; in some column one appears exactly 16 times; every dp index appears in some column.
All inputs are finite; a program needn't handle non-finite values.
Results may differ from a plain program's by a relative error of at most 0.039.
Values may be sent and summed in bfloat16 or wider, within the bound.
A program may use at most 192 MiB of HBM per device.

v0:
```python
import jax
import jax.numpy as jnp
from jax import lax
from jax.sharding import PartitionSpec as P

BS = 256
ORTHO_STEPS = 8


damping = 0.1
highest = lax.Precision.HIGHEST


def from_root(value, axis, source):
    kept = jnp.where(lax.axis_index(axis) == source, value, 0).astype(value.dtype)
    return lax.psum(kept, axis)


def refresh_blocks(moment, old_basis):
    rounded = moment.astype(jnp.bfloat16)
    product = jnp.einsum("sij,sjk->sik", rounded, old_basis, preferred_element_type=jnp.float32)
    frobenius = jnp.sqrt(jnp.sum(product * product, axis=(1, 2), keepdims=True) + 1e-06)
    current = product / frobenius
    for counter in range(ORTHO_STEPS):
        gram_matrix = jnp.einsum("sji,sjk->sik", current, current, precision=highest)
        current = 1.5 * current - 0.5 * jnp.einsum(
            "sij,sjk->sik", current, gram_matrix, precision=highest
        )
    applied = jnp.einsum("sij,sjk->sik", moment, current, precision=highest)
    values = jnp.mean(applied * current, axis=1) / (jnp.mean(current * current, axis=1) + 1e-06)
    return (current.astype(jnp.bfloat16), values.astype(jnp.bfloat16))


def feature_moments(values, tok_count):
    split_rows = values.reshape(tok_count, values.shape[1] // BS, BS)
    return jnp.einsum("tai,taj->aij", split_rows, split_rows, preferred_element_type=jnp.float32)


def shards(acts, out_grads, weight_grad, old_bases, owner_table):
    tok_count = acts.shape[0]
    data_size = lax.axis_size("dp")
    owner_size = lax.axis_size("owner")
    blocks_a = acts.shape[1] // BS
    count_all = blocks_a + out_grads.shape[1] // BS
    slot_count = old_bases.shape[2]
    total_tokens = tok_count * data_size
    partial_value = jnp.concatenate(
        [feature_moments(acts, tok_count), feature_moments(out_grads, tok_count)], axis=0
    ).astype(jnp.bfloat16)
    owners = owner_table[0, :, 0]
    block_order = jnp.arange(count_all, dtype=jnp.int32)
    same_owner = owners[:, None] == owners[None, :]
    slot_ranks = jnp.sum(
        jnp.where(same_owner & (block_order[:, None] < block_order[None, :]), 1, 0), axis=0
    ).astype(jnp.int32)
    to_owner = owners[None, None, :] == jnp.arange(data_size, dtype=jnp.int32)[:, None, None]
    to_slot = slot_ranks[None, None, :] == jnp.arange(slot_count, dtype=jnp.int32)[None, :, None]
    target = (to_owner & to_slot).astype(jnp.bfloat16)
    outgoing = jnp.einsum(
        "dkb,bij->dkij", target, partial_value, preferred_element_type=jnp.float32
    ).astype(jnp.bfloat16)
    summed = lax.psum_scatter(outgoing, "dp", scatter_dimension=0, tiled=True).astype(jnp.float32)
    refreshed, values = refresh_blocks(summed[0] / total_tokens, old_bases[0, 0])
    new_bases = refreshed[None, None]
    new_values = values[None, None]
    gathered, held_values = (
        lax.all_gather(refreshed, "dp", axis=0, tiled=True),
        lax.all_gather(values, "dp", axis=0, tiled=True),
    )
    places = owners * slot_count + slot_ranks
    chosen = (
        places[:, None] == jnp.arange(data_size * slot_count, dtype=jnp.int32)[None, :]
    ).astype(jnp.bfloat16)
    blocks = jnp.einsum("bs,sij->bij", chosen, gathered, preferred_element_type=jnp.float32).astype(
        jnp.bfloat16
    )
    block_values = jnp.dot(chosen, held_values, preferred_element_type=jnp.float32).astype(
        jnp.bfloat16
    )
    left_basis = blocks[:blocks_a]
    left_values = block_values[:blocks_a].astype(jnp.float32)
    source_column = lax.axis_index("dp") * owner_size // data_size
    width_g = weight_grad.shape[1] // BS
    first_block = blocks_a + lax.axis_index("dp") % (data_size // owner_size) * width_g
    needed_basis = lax.dynamic_slice_in_dim(blocks, first_block, width_g, 0)
    needed_values = lax.dynamic_slice_in_dim(block_values, first_block, width_g, 0)
    right_basis, far_values = (
        from_root(needed_basis, "owner", source_column),
        from_root(needed_values, "owner", source_column),
    )
    right_values = far_values.astype(jnp.float32)
    grad_tiles = weight_grad.reshape(blocks_a, BS, width_g, BS)
    turned = jnp.einsum(
        "aik,aigj->akgj", left_basis, grad_tiles, preferred_element_type=jnp.float32
    ).astype(jnp.bfloat16)
    rotated = jnp.einsum("akgj,gjl->akgl", turned, right_basis, preferred_element_type=jnp.float32)
    divisor = left_values[:, :, None, None] * right_values[None, None, :, :] + damping
    scaled = (rotated / divisor).astype(jnp.bfloat16)
    returned = jnp.einsum(
        "akgl,gjl->akgj", scaled, right_basis, preferred_element_type=jnp.float32
    ).astype(jnp.bfloat16)
    result = jnp.einsum(
        "aik,akgj->aigj", left_basis, returned, preferred_element_type=jnp.float32
    ).astype(jnp.bfloat16)
    return (result.reshape(weight_grad.shape), new_bases, new_values)


def solution(mesh):
    placed = (
        P(("groups", "dp"), "owner"),
        P(("groups", "dp"), "owner"),
        P(("groups", "owner"), "dp"),
        P(("groups", "owner"), "dp", None, None, None),
        P("owner", None, None),
    )
    return jax.shard_map(
        shards,
        mesh=mesh,
        in_specs=placed,
        out_specs=(
            P(("groups", "owner"), "dp"),
            P(("groups", "owner"), "dp", None, None, None),
            P(("groups", "owner"), "dp", None, None),
        ),
        check_vma=False,
    )
```

profile of v0, /device:TPU:0, one launch (start us, length us, event | category | flops | bytes accessed | tf_op | source)
XLA Modules:
  0.0 487.8 jit_solution(17980168451615916047)
XLA Ops:
  8.8 4.6 copy.43
  17.3 10.7 %fusion.43 = bf16[24,256,256]{2,1,0:T(8,128)(2,1)S(1)} fusion(bf16[128,24,8,256]{3,2,1,0:T(8,128)(2,1)} %bitcast.94), kind=kOutput, calls=%fused_computation.41 | convolution fusion | flops 3222798336 | bytes 15728640 | tf_op jit(solution)/shard_map/tai,taj->aij/dot_general | solution.py:36
  28.3 6.1 %convolution_convert_fusion = bf16[4,16,256,256]{3,1,2,0:T(8,128)(2,1)} fusion(bf16[30,256,256]{2,1,0:T(8,128)(2,1)S(1)} %pad_maximum_fusion, pred[16,30]{1,0:T(8,128)(4,1)S(1)} %iota_compare_fusion.3, pred[4,30]{1,0:T(4,128)(4,1)S(1)} %iota_compare_fusion.4), kind=kOutput, calls=%fused_computation.18 | convolution fusion | flops 255854464 | bytes 12321368 | tf_op jit(solution)/shard_map/dkb,bij->dkij/dot_general | solution.py:59
  34.6 74.3 %reduce-scatter.2.cloned.1.call-done = bf16[1,16,256,256]{3,1,2,0:T(8,128)(2,1)} async-done(((bf16[4,16,256,256]{3,1,2,0:T(8,128)(2,1)}), bf16[1,16,256,256]{3,1,2,0:T(8,128)(2,1)}) %reduce-scatter.2.cloned.1.call-update) | async-done | bytes 2097168 | tf_op jit(solution)/shard_map/reduce_scatter | solution.py:62
  114.3 7.2 %fusion.50 = f32[16,256,256]{2,1,0:T(8,128)S(1)} fusion(f32[16,256,256]{2,1,0:T(8,128)S(1)} %get-tuple-element.8, f32[16]{0:T(128)S(1)} %add_sqrt_fusion), kind=kOutput, calls=%fused_computation.50 | convolution fusion | flops 3222274048 | bytes 8388672 | tf_op jit(solution)/shard_map/sji,sjk->sik/dot_general | solution.py:25
  121.5 5.1 %multiply_subtract_fusion.7 = f32[16,256,256]{2,1,0:T(8,128)S(1)} fusion(f32[16,256,256]{2,1,0:T(8,128)S(1)} %fusion.50, f32[16,256,256]{2,1,0:T(8,128)S(1)} %get-tuple-element.8, f32[16]{0:T(128)S(1)} %add_sqrt_fusion), kind=kOutput, calls=%fused_computation.32 | convolution fusion | flops 3226468352 | bytes 12582976 | tf_op jit(solution)/shard_map/sij,sjk->sik/dot_general | solution.py:26
  126.7 6.8 %fusion.63 = f32[16,256,256]{2,1,0:T(8,128)S(1)} fusion(f32[16,256,256]{2,1,0:T(8,128)S(1)} %multiply_subtract_fusion.7), kind=kOutput, calls=%fused_computation.72 | convolution fusion | flops 3221225472 | bytes 8388608 | tf_op jit(solution)/shard_map/sji,sjk->sik/dot_general | solution.py:25
  133.5 5.3 %multiply_subtract_fusion.6 = f32[16,256,256]{2,1,0:T(8,128)S(1)} fusion(f32[16,256,256]{2,1,0:T(8,128)S(1)} %multiply_subtract_fusion.7, f32[16,256,256]{2,1,0:T(8,128)S(1)} %fusion.63), kind=kOutput, calls=%fused_computation.31 | convolution fusion | flops 3224371200 | bytes 12582912 | tf_op jit(solution)/shard_map/sij,sjk->sik/dot_general | solution.py:26
  138.7 6.8 %fusion.64 = f32[16,256,256]{2,1,0:T(8,128)S(1)} fusion(f32[16,256,256]{2,1,0:T(8,128)S(1)} %multiply_subtract_fusion.6), kind=kOutput, calls=%fused_computation.73 | convolution fusion | flops 3221225472 | bytes 8388608 | tf_op jit(solution)/shard_map/sji,sjk->sik/dot_general | solution.py:25
  145.5 5.0 %multiply_subtract_fusion.5 = f32[16,256,256]{2,1,0:T(8,128)S(1)} fusion(f32[16,256,256]{2,1,0:T(8,128)S(1)} %multiply_subtract_fusion.6, f32[16,256,256]{2,1,0:T(8,128)S(1)} %fusion.64), kind=kOutput, calls=%fused_computation.30 | convolution fusion | flops 3224371200 | bytes 12582912 | tf_op jit(solution)/shard_map/sij,sjk->sik/dot_general | solution.py:26
  150.6 6.8 %fusion.65 = f32[16,256,256]{2,1,0:T(8,128)S(1)} fusion(f32[16,256,256]{2,1,0:T(8,128)S(1)} %multiply_subtract_fusion.5), kind=kOutput, calls=%fused_computation.74 | convolution fusion | flops 3221225472 | bytes 8388608 | tf_op jit(solution)/shard_map/sji,sjk->sik/dot_general | solution.py:25
  157.4 5.1 %multiply_subtract_fusion.4 = f32[16,256,256]{2,1,0:T(8,128)S(1)} fusion(f32[16,256,256]{2,1,0:T(8,128)S(1)} %multiply_subtract_fusion.5, f32[16,256,256]{2,1,0:T(8,128)S(1)} %fusion.65), kind=kOutput, calls=%fused_computation.29 | convolution fusion | flops 3224371200 | bytes 12582912 | tf_op jit(solution)/shard_map/sij,sjk->sik/dot_general | solution.py:26
  162.5 6.8 %fusion.66 = f32[16,256,256]{2,1,0:T(8,128)S(1)} fusion(f32[16,256,256]{2,1,0:T(8,128)S(1)} %multiply_subtract_fusion.4), kind=kOutput, calls=%fused_computation.75 | convolution fusion | flops 3221225472 | bytes 8388608 | tf_op jit(solution)/shard_map/sji,sjk->sik/dot_general | solution.py:25
  169.3 5.3 %multiply_subtract_fusion.3 = f32[16,256,256]{2,1,0:T(8,128)S(1)} fusion(f32[16,256,256]{2,1,0:T(8,128)S(1)} %multiply_subtract_fusion.4, f32[16,256,256]{2,1,0:T(8,128)S(1)} %fusion.66), kind=kOutput, calls=%fused_computation.28 | convolution fusion | flops 3224371200 | bytes 12582912 | tf_op jit(solution)/shard_map/sij,sjk->sik/dot_general | solution.py:26
  174.6 6.8 %fusion.67 = f32[16,256,256]{2,1,0:T(8,128)S(1)} fusion(f32[16,256,256]{2,1,0:T(8,128)S(1)} %multiply_subtract_fusion.3), kind=kOutput, calls=%fused_computation.76 | convolution fusion | flops 3221225472 | bytes 8388608 | tf_op jit(solution)/shard_map/sji,sjk->sik/dot_general | solution.py:25
  181.4 5.0 %multiply_subtract_fusion.2 = f32[16,256,256]{2,1,0:T(8,128)S(1)} fusion(f32[16,256,256]{2,1,0:T(8,128)S(1)} %multiply_subtract_fusion.3, f32[16,256,256]{2,1,0:T(8,128)S(1)} %fusion.67), kind=kOutput, calls=%fused_computation.27 | convolution fusion | flops 3224371200 | bytes 12582912 | tf_op jit(solution)/shard_map/sij,sjk->sik/dot_general | solution.py:26
  186.4 6.8 %fusion.68 = f32[16,256,256]{2,1,0:T(8,128)S(1)} fusion(f32[16,256,256]{2,1,0:T(8,128)S(1)} %multiply_subtract_fusion.2), kind=kOutput, calls=%fused_computation.77 | convolution fusion | flops 3221225472 | bytes 8388608 | tf_op jit(solution)/shard_map/sji,sjk->sik/dot_general | solution.py:25
  193.2 5.3 %multiply_subtract_fusion.1 = f32[16,256,256]{2,1,0:T(8,128)S(1)} fusion(f32[16,256,256]{2,1,0:T(8,128)S(1)} %multiply_subtract_fusion.2, f32[16,256,256]{2,1,0:T(8,128)S(1)} %fusion.68), kind=kOutput, calls=%fused_computation.26 | convolution fusion | flops 3224371200 | bytes 12582912 | tf_op jit(solution)/shard_map/sij,sjk->sik/dot_general | solution.py:26
  198.5 6.8 %fusion.69 = f32[16,256,256]{2,1,0:T(8,128)S(1)} fusion(f32[16,256,256]{2,1,0:T(8,128)S(1)} %multiply_subtract_fusion.1), kind=kOutput, calls=%fused_computation.78 | convolution fusion | flops 3221225472 | bytes 8388608 | tf_op jit(solution)/shard_map/sji,sjk->sik/dot_general | solution.py:25
  205.3 6.5 %fusion.62 = (bf16[16,256,256]{2,1,0:T(8,128)(2,1)}, f32[16,256]{1,0:T(8,128)S(1)}, f32[16,256,256]{2,1,0:T(8,128)}) fusion(f32[16,256,256]{2,1,0:T(8,128)S(1)} %multiply_subtract_fusion.1, f32[16,256,256]{2,1,0:T(8,128)S(1)} %fusion.69), kind=kOutput, calls=%fused_computation.71 | convolution fusion | flops 3227512832 | bytes 14696448 | tf_op jit(solution)/shard_map/sij,sjk->sik/dot_general | solution.py:26
  212.0 19.5 %copy.91 = bf16[192,8,24,256]{3,2,1,0:T(8,128)(2,1)} copy(bf16[192,8,24,256]{3,1,2,0:T(8,128)(2,1)} %bitcast.89) | data formatting | bytes 37748736
  231.5 11.4 %multiply_reduce_fusion.1 = f32[16,256]{1,0:T(8,128)S(1)} fusion(f32[16,256,256]{2,1,0:T(8,128)} %get-tuple-element.9, f32[16,256,256]{2,0,1:T(8,128)} %get-tuple-element.5), kind=kOutput, calls=%fused_computation.24 | convolution fusion | flops 3223318528 | bytes 8404992 | tf_op jit(solution)/shard_map/sij,sjk->sik/dot_general | solution.py:29
  243.0 5.3 %all_gather.7 = bf16[64,256]{1,0:T(8,128)(2,1)S(1)} all-gather(bf16[16,256]{1,0:T(8,128)(2,1)S(1)} %divide_convert_fusion), channel_id=1, replica_groups=mesh['groups'=2,'dp'=4,'owner'=4] {'dp'}, dimensions={0}, use_global_device_ids=true | all-gather | bytes 40960 | tf_op jit(solution)/shard_map/all_gather | solution.py:68
  248.3 22.1 %all-gather.2.cloned.1.call-done = bf16[64,256,256]{2,1,0:T(8,128)(2,1)} async-done(((bf16[16,256,256]{2,1,0:T(8,128)(2,1)}), bf16[64,256,256]{2,1,0:T(8,128)(2,1)}) %all-gather.2.cloned.1.call-update) | async-done | bytes 8388624 | tf_op jit(solution)/shard_map/all_gather | solution.py:67
  270.4 9.3 %fusion.38 = bf16[30,256,256]{2,0,1:T(8,128)(2,1)S(1)} fusion(bf16[64,256,256]{2,1,0:T(8,128)(2,1)} %all-gather.2.cloned.1.call-done, s32[30]{0:T(128)S(1)} %multiply_add_fusion), kind=kOutput, calls=%fused_computation.40 | convolution fusion | flops 253626240 | bytes 12320888 | tf_op jit(solution)/shard_map/bs,sij->bij/dot_general | solution.py:74
  284.4 19.6 %psum.15 = bf16[24,256]{1,0:T(8,128)(2,1)S(1)} all-reduce(bf16[24,256]{1,0:T(8,128)(2,1)S(1)} %slice_select_fusion.1), channel_id=1, replica_groups=mesh['groups'=2,'dp'=4,'owner'=4] {'owner'}, use_global_device_ids=true, to_apply=%region_6.7 | all-reduce | flops 6144 | bytes 24576 | tf_op jit(solution)/shard_map/psum | solution.py:16
  305.3 19.1 %fusion.17 = bf16[6,256,24,256]{3,1,2,0:T(8,128)(2,1)} fusion(bf16[6,256,24,256]{3,2,1,0:T(8,128)(2,1)} %bitcast.87, bf16[6,256,256,1]{2,0,1,3:T(8,128)(2,1)S(1)} %slice_bitcast_fusion), kind=kOutput, calls=%fused_computation.14 | convolution fusion | flops 4841275392 | bytes 38535168 | tf_op jit(solution)/shard_map/aik,aigj->akgj/dot_general | solution.py:93
  324.4 81.4 %all-reduce.2.cloned.1.call-done = bf16[24,256,256]{2,0,1:T(8,128)(2,1)} async-done(((bf16[24,256,256]{2,0,1:T(8,128)(2,1)}), bf16[24,256,256]{2,0,1:T(8,128)(2,1)}) %all-reduce.2.cloned.1.call-update) | async-done | bytes 3145744 | tf_op jit(solution)/shard_map/psum | solution.py:16
  405.8 20.2 %fusion = bf16[6,256,24,256]{1,3,0,2:T(8,128)(2,1)} fusion(f32[24,256]{1,0:T(8,128)S(1)} %convert_element_type.68, f32[6,256]{1,0:T(8,128)S(1)} %slice_convert_fusion, bf16[6,256,24,256]{3,1,2,0:T(8,128)(2,1)} %fusion.17, bf16[24,256,256,1]{2,0,1,3:T(8,128)(2,1)} %bitcast.95), kind=kOutput, calls=%fused_computation.1 | convolution fusion | flops 4869586944 | bytes 40925184 | tf_op jit(solution)/shard_map/akgj,gjl->akgl/dot_general | solution.py:96
  426.1 20.5 %fusion.20 = bf16[6,256,24,256]{3,1,2,0:T(8,128)(2,1)} fusion(bf16[6,256,24,256]{1,3,0,2:T(8,128)(2,1)} %fusion, bf16[24,256,256]{2,0,1:T(8,128)(2,1)} %all-reduce.2.cloned.1.call-done, bf16[6,256,256,1]{2,0,1,3:T(8,128)(2,1)S(1)} %slice_bitcast_fusion), kind=kOutput, calls=%fused_computation.15 | convolution fusion | flops 9682550784 | bytes 41680896 | tf_op jit(solution)/shard_map/aik,akgj->aigj/dot_general | solution.py:102
  446.6 17.9 %copy.67 = bf16[6,256,24,256]{3,2,1,0:T(8,128)(2,1)S(1)} copy(bf16[6,256,24,256]{3,1,2,0:T(8,128)(2,1)} %fusion.20) | data formatting | bytes 37748736 | tf_op jit(solution)/shard_map/convert_element_type | solution.py:104
  464.6 16.5 %copy.92 = bf16[192,8,24,256]{3,1,2,0:T(8,128)(2,1)} copy(bf16[192,8,24,256]{3,2,1,0:T(8,128)(2,1)S(1)} %bitcast.88) | data formatting | bytes 37748736
  (32 shorter events, 17.6 us)
Async XLA Ops:
  7.2 106.1 %copy-start = (bf16[1,1,16,256,256]{4,3,2,1,0:T(8,128)(2,1)S(1)}, bf16[1,1,16,256,256]{4,3,2,1,0:T(8,128)(2,1)}, u32[]{:S(2)}) copy-start(bf16[1,1,16,256,256]{4,3,2,1,0:T(8,128)(2,1)} %param.8) | copy-start | bytes 6291460
  7.2 101.8 %reduce-scatter.2.cloned.1.call-start = ((), (), s32[]{:S(2)}) async-start(), calls=%async_computation.1 | async-start | bytes 10485760 | tf_op jit(solution)/shard_map/reduce_scatter | solution.py:62
  34.4 236.0 %all-gather.2.cloned.1.call-start = ((), (), s32[]{:S(2)}) async-start(), calls=%async_computation.2 | async-start | bytes 10485760 | tf_op jit(solution)/shard_map/all_gather | solution.py:67
  211.8 194.0 %all-reduce.2.cloned.1.call-start = ((), (), s32[]{:S(2)}) async-start(), calls=%async_computation.3 | async-start | bytes 6291456 | tf_op jit(solution)/shard_map/psum | solution.py:16
  212.0 19.5 %copy-start.4 = (s32[1,30,1]{1,2,0:T(1,128)S(1)}, s32[1,30,1]{1,2,0:T(1,128)}, u32[]{:S(2)}) copy-start(s32[1,30,1]{1,2,0:T(1,128)} %param.9) | copy-start | bytes 364
  243.0 36.7 %copy-start.3 = (bf16[16,256]{1,0:T(8,128)(2,1)}, bf16[16,256]{1,0:T(8,128)(2,1)S(1)}, u32[]{:S(2)}) copy-start(bf16[16,256]{1,0:T(8,128)(2,1)S(1)} %divide_convert_fusion) | copy-start | bytes 24580
  279.7 1.9 copy-start.2
  464.5 16.5 %copy-start.1 = (bf16[1,1,16,256,256]{4,3,2,1,0:T(8,128)(2,1)S(1)}, bf16[1,1,16,256,256]{4,3,2,1,0:T(8,128)(2,1)}, u32[]{:S(2)}) copy-start(bf16[1,1,16,256,256]{4,3,2,1,0:T(8,128)(2,1)} %param.8) | copy-start | bytes 6291460
Sparse Core Ops, SparseCore 0:
  34.5 74.3 reduce-scatter.1
  211.9 58.4 all-gather.1
  284.3 121.4 all-reduce.1
where the time goes:
time: 494 us; the launch traced here: 488 us
  matrix products  200 us (40%)
  waiting for transfers between devices  178 us (36%)
  local copies, waits for them, and re-layouts  61.8 us (13%)
  blocking collectives  24.9 us (5%)
  between operations  14.3 us (3%)
  other arithmetic  8.8 us (2%)
    psum x1, waiting for transfers between devices, from_root(): return lax.psum(kept, axis)  81.4 us
    reduce_scatter x1, waiting for transfers between devices, shards(): lax.psum_scatter(outgoing, 'dp', scatter_dimension=0, tiled=True)  74.3 us
    dot_general x8, matrix products, refresh_blocks(): jnp.einsum('sji,sjk->sik', current, current, precision=highest)  54.7 us
    dot_general x8, matrix products, refresh_blocks(): jnp.einsum('sij,sjk->sik', current, gram_matrix, precision=highest)  42.6 us
    unnamed x13, local copies, waits for them, and re-layouts  42.5 us
    all_gather x1, waiting for transfers between devices, shards(): lax.all_gather(refreshed, 'dp', axis=0, tiled=True)  22.1 us
    dot_general x1, matrix products, shards(): jnp.einsum('aik,akgj->aigj', left_basis, returned, preferred_element_type...  20.5 us
    dot_general x1, matrix products, shards(): jnp.einsum('akgj,gjl->akgl', turned, right_basis, preferred_element_type=...  20.2 us
  transfers between devices with their start and end apart: 3, of which 3 were waited for; matrix products, arithmetic and copies ran while one was open for 11% of the time, Pallas kernels for 0%

commit v1 on v0

v1 whole, which is shorter than its diff:
```python
import functools

import jax
import jax.numpy as jnp
from jax import lax
from jax.experimental import pallas as pl
from jax.experimental.pallas import tpu as pltpu
from jax.sharding import PartitionSpec as P

BS = 256
ROWS = BS + 16
ORTHO_STEPS = 8
DAMPING = 0.1
F32 = jnp.float32
BF16 = jnp.bfloat16
MIB = 1 << 20


def dot(a, b, contract):
    return lax.dot_general(a, b, (contract, ((), ())), preferred_element_type=F32)


def ceil_div(a, b):
    return -(-a // b)


def moments_kernel(places_a, old_slot, held, acts_ref, grads_ref, old_ref, mom_ref, old_out_ref):
    step = pl.program_id(0)
    is_left = places_a[step] == 1

    @pl.when(is_left)
    def _():
        x = acts_ref[...]
        mom_ref[0] = dot(x, x, ((0,), (0,))).astype(BF16)

    @pl.when(jnp.logical_not(is_left))
    def _():
        x = grads_ref[...]
        mom_ref[0] = dot(x, x, ((0,), (0,))).astype(BF16)

    old_out_ref[0] = jnp.where(held[step] == 1, old_ref[0], jnp.zeros_like(old_ref[0]))


def moments(acts, grads, old, is_left, block_a, block_g, old_slot, held):
    tokens = acts.shape[0]
    count = is_left.shape[0]

    def kernel(is_left, block_a, block_g, old_slot, held, *refs):
        moments_kernel(is_left, old_slot, held, *refs)

    return pl.pallas_call(
        kernel,
        grid_spec=pltpu.PrefetchScalarGridSpec(
            num_scalar_prefetch=5,
            grid=(count,),
            in_specs=[
                pl.BlockSpec((tokens, BS), lambda i, l, a, g, s, h: (0, a[i])),
                pl.BlockSpec((tokens, BS), lambda i, l, a, g, s, h: (0, g[i])),
                pl.BlockSpec((1, BS, BS), lambda i, l, a, g, s, h: (s[i], 0, 0)),
            ],
            out_specs=[
                pl.BlockSpec((1, BS, BS), lambda i, l, a, g, s, h: (i, 0, 0)),
                pl.BlockSpec((1, BS, BS), lambda i, l, a, g, s, h: (i, 0, 0)),
            ],
        ),
        out_shape=[jax.ShapeDtypeStruct((count, BS, BS), BF16)] * 2,
        compiler_params=pltpu.CompilerParams(vmem_limit_bytes=32 * MIB),
        cost_estimate=pl.CostEstimate(
            flops=2 * count * tokens * BS * BS, bytes_accessed=24 * MIB, transcendentals=0
        ),
        name="moments",
    )(is_left, block_a, block_g, old_slot, held, acts, grads, old)


def reduce_kernel(n, slots, mom, old, mom_out, old_out, near, far, own, near_send, near_recv, far_send, far_recv):
    me = lax.axis_index("dp")
    pairs = n // 2
    chip, core = me // 2, lax.rem(me, 2)
    partner = chip * 2 + (1 - core)

    barrier = pltpu.get_barrier_semaphore()
    pl.semaphore_signal(barrier, inc=1, device_id={"dp": partner})
    for k in range(1, pairs):
        there = lax.rem(chip + k, pairs) * 2 + core
        pl.semaphore_signal(barrier, inc=1, device_id={"dp": there})
    pl.semaphore_wait(barrier, pairs)

    def to_partner(k, part):
        target = lax.rem(chip + k, pairs) * 2 + (1 - core)
        return pltpu.make_async_remote_copy(
            src_ref=(old, mom)[part].at[target],
            dst_ref=near.at[k - 1, part],
            send_sem=near_send.at[k - 1, part],
            recv_sem=near_recv.at[k - 1, part],
            device_id={"dp": partner},
        )

    def to_chip(k, part):
        return pltpu.make_async_remote_copy(
            src_ref=own.at[k - 1, part],
            dst_ref=far.at[k - 1, part],
            send_sem=far_send.at[k - 1, part],
            recv_sem=far_recv.at[k - 1, part],
            device_id={"dp": lax.rem(chip + k, pairs) * 2 + core},
        )

    order = [(k, part) for part in (0, 1) for k in range(1, pairs + 1)]
    for k, part in order:
        to_partner(k, part).start()
    for k, part in order:
        to_partner(k, part).wait()
        source = (old, mom)[part]
        mine = lax.rem(chip + k, pairs) * 2 + core

        @pl.loop(0, slots)
        def _(s):
            own[k - 1, part, s] = (
                source[mine, s].astype(F32) + near[k - 1, part, s].astype(F32)
            ).astype(BF16)

        if k < pairs:
            to_chip(k, part).start()
    for part in (0, 1):
        for k in range(1, pairs):
            to_chip(k, part).wait()

        @pl.loop(0, slots)
        def _(s):
            total = own[pairs - 1, part, s].astype(F32)
            for k in range(1, pairs):
                total = total + far[k - 1, part, s].astype(F32)
            if part == 0:
                old_out[s] = total.astype(BF16)
            else:
                mom_out[s] = total


def reduce_blocks(n, slots, mom, old):
    pairs = n // 2
    vmem = pl.BlockSpec(memory_space=pltpu.VMEM)
    buffer = pltpu.VMEM((pairs, 2, slots, BS, BS), BF16)
    return pl.pallas_call(
        functools.partial(reduce_kernel, n, slots),
        out_shape=[
            jax.ShapeDtypeStruct((slots, BS, BS), F32),
            jax.ShapeDtypeStruct((slots, BS, BS), BF16),
        ],
        in_specs=[vmem, vmem],
        out_specs=[vmem, vmem],
        scratch_shapes=[buffer] * 3 + [pltpu.SemaphoreType.DMA((pairs, 2))] * 4,
        compiler_params=pltpu.CompilerParams(
            collective_id=0, has_side_effects=True, vmem_limit_bytes=56 * MIB
        ),
        cost_estimate=pl.CostEstimate(flops=10 * MIB, bytes_accessed=16 * MIB, transcendentals=0),
        name="reduce_blocks",
    )(mom, old)


def refresh_kernel(group, tokens, mom_ref, old_ref, out_ref, current):
    for s in range(group):
        moment = mom_ref[s] * (1.0 / tokens)
        product = dot(moment.astype(BF16), old_ref[s], ((1,), (0,)))
        current[s] = product / jnp.sqrt(jnp.sum(product * product) + 1e-06)

    @pl.loop(0, ORTHO_STEPS)
    def _(step):
        rounded = [current[s].astype(BF16) for s in range(group)]
        grams = [dot(y, y, ((0,), (0,))).astype(BF16) for y in rounded]
        for s in range(group):
            current[s] = 1.5 * current[s] - 0.5 * dot(rounded[s], grams[s], ((1,), (0,)))

    for s in range(group):
        moment = mom_ref[s] * (1.0 / tokens)
        high = moment.astype(BF16)
        low = (moment - high.astype(F32)).astype(BF16)
        y = current[s]
        basis = y.astype(BF16)
        applied = dot(high, basis, ((1,), (0,))) + dot(low, basis, ((1,), (0,)))
        top = jnp.mean(applied * y, axis=0, keepdims=True)
        value = top / (jnp.mean(y * y, axis=0, keepdims=True) + 1e-06)
        out_ref[s, 0:BS] = basis
        out_ref[s, BS:ROWS] = jnp.broadcast_to(value, (ROWS - BS, BS)).astype(BF16)


def refresh(mom, old, tokens):
    slots = mom.shape[0]
    group = 4 if slots % 4 == 0 else (2 if slots % 2 == 0 else 1)
    block = pl.BlockSpec((group, BS, BS), lambda i: (i, 0, 0))
    return pl.pallas_call(
        functools.partial(refresh_kernel, group, tokens),
        grid=(slots // group,),
        in_specs=[block, block],
        out_specs=pl.BlockSpec((group, ROWS, BS), lambda i: (i, 0, 0)),
        out_shape=jax.ShapeDtypeStruct((slots, ROWS, BS), BF16),
        scratch_shapes=[pltpu.VMEM((group, BS, BS), F32)],
        compiler_params=pltpu.CompilerParams(vmem_limit_bytes=32 * MIB),
        cost_estimate=pl.CostEstimate(
            flops=36 * slots * BS**3, bytes_accessed=8 * MIB, transcendentals=0
        ),
        name="refresh",
    )(mom, old)


def spread_kernel(
    n, columns, left, fresh, column_blocks, right, held, up_send, up_recv, down_send, down_recv,
    give_send, give_recv, all_send, all_recv, local_sem,
):
    me, here = lax.axis_index("dp"), lax.axis_index("owner")
    per = n // columns
    above = jnp.minimum(here + 1, columns - 1)
    below = jnp.maximum(here - 1, 0)
    has_above, has_below = here < columns - 1, here > 0

    barrier = pltpu.get_barrier_semaphore()
    for k in range(1, n):
        pl.semaphore_signal(barrier, inc=1, device_id={"dp": lax.rem(me + k, n)})

    @pl.when(has_above)
    def _():
        pl.semaphore_signal(barrier, inc=1, device_id={"owner": above})

    @pl.when(has_below)
    def _():
        pl.semaphore_signal(barrier, inc=1, device_id={"owner": below})

    pl.semaphore_wait(barrier, n - 1 + jnp.where(has_above, 1, 0) + jnp.where(has_below, 1, 0))

    held[here] = fresh[left:]

    def along(k, column, send, recv, there):
        return pltpu.make_async_remote_copy(
            src_ref=held.at[column],
            dst_ref=held.at[column],
            send_sem=send.at[k],
            recv_sem=recv.at[k],
            device_id={"owner": there},
        )

    def clamp(column):
        return jnp.clip(column, 0, columns - 1)

    def up(k, column):
        return along(k, clamp(column), up_send, up_recv, above)

    def down(k, column):
        return along(k, clamp(column), down_send, down_recv, below)

    def give(column, target):
        return pltpu.make_async_remote_copy(
            src_ref=held.at[column],
            dst_ref=right.at[me],
            send_sem=give_send.at[target],
            recv_sem=give_recv.at[me],
            device_id={"dp": target},
        )

    def taken(source):
        return pltpu.make_async_remote_copy(
            src_ref=held.at[0],
            dst_ref=right.at[source],
            send_sem=give_send.at[source],
            recv_sem=give_recv.at[source],
            device_id={"dp": source},
        )

    def keep(column):
        return pltpu.make_async_copy(held.at[column], right.at[me], local_sem.at[0])

    def share(column):
        for h in range(per):
            target = column * per + h

            @pl.when(target != me)
            def _():
                give(column, target).start()

            @pl.when(target == me)
            def _():
                keep(column).start()

    def to_all(k):
        return pltpu.make_async_remote_copy(
            src_ref=fresh,
            dst_ref=column_blocks.at[me],
            send_sem=all_send.at[k - 1],
            recv_sem=all_recv.at[k - 1],
            device_id={"dp": lax.rem(me + k, n)},
        )

    def from_all(k):
        return pltpu.make_async_remote_copy(
            src_ref=fresh,
            dst_ref=column_blocks.at[lax.rem(me + n - k, n)],
            send_sem=all_send.at[k - 1],
            recv_sem=all_recv.at[k - 1],
            device_id={"dp": lax.rem(me + k, n)},
        )

    mine = pltpu.make_async_copy(fresh, column_blocks.at[me], local_sem.at[1])
    for k in range(columns - 1):
        sends_up = has_above & (here - k >= 0)
        sends_down = has_below & (here + k <= columns - 1)

        @pl.when(sends_up)
        def _():
            up(k, here - k).start()

        @pl.when(sends_down)
        def _():
            down(k, here + k).start()

        if k == 0:
            share(here)
            mine.start()
            for j in range(1, n):
                to_all(j).start()

        @pl.when(here - 1 - k >= 0)
        def _():
            up(k, here - 1 - k).wait_recv()
            share(clamp(here - 1 - k))

        @pl.when(here + 1 + k <= columns - 1)
        def _():
            down(k, here + 1 + k).wait_recv()
            share(clamp(here + 1 + k))

    for k in range(columns - 1):

        @pl.when(has_above & (here - k >= 0))
        def _():
            up(k, here - k).wait_send()

        @pl.when(has_below & (here + k <= columns - 1))
        def _():
            down(k, here + k).wait_send()

    mine.wait()
    keep(here).wait()
    for k in range(1, n):
        to_all(k).wait_send()
        from_all(k).wait_recv()
        other = lax.rem(me + k, n)
        taken(other).wait_send()
        taken(other).wait_recv()


def spread(n, columns, left, fresh):
    slots = fresh.shape[0]
    dma = pltpu.SemaphoreType.DMA
    vmem = pl.BlockSpec(memory_space=pltpu.VMEM)
    return pl.pallas_call(
        functools.partial(spread_kernel, n, columns, left),
        out_shape=[
            jax.ShapeDtypeStruct((n, slots, ROWS, BS), BF16),
            jax.ShapeDtypeStruct((n, slots - left, ROWS, BS), BF16),
        ],
        in_specs=[vmem],
        out_specs=[vmem, vmem],
        scratch_shapes=[pltpu.VMEM((columns, slots - left, ROWS, BS), BF16)]
        + [dma((columns - 1,))] * 4
        + [dma((n,))] * 2
        + [dma((n - 1,))] * 2
        + [dma((2,))],
        compiler_params=pltpu.CompilerParams(
            collective_id=1, has_side_effects=True, vmem_limit_bytes=56 * MIB
        ),
        cost_estimate=pl.CostEstimate(flops=0, bytes_accessed=16 * MIB, transcendentals=0),
        name="spread",
    )(fresh)


def precondition_kernel(
    chunk, place, used, grad_ref, left_ref, la_ref, right_ref, block_ref, out_ref, bases_ref, turned_left
):
    row, part = pl.program_id(0), pl.program_id(1)
    slot = jnp.minimum(row * pl.num_programs(1) + part, used.shape[0] - 1)

    @pl.when(part == 0)
    def _():
        turned_left[...] = left_ref[0, 0:BS].T

    left = left_ref[0, 0:BS]
    la = la_ref[0][:, 0:1]
    for j in range(chunk):
        cols = slice(j * BS, (j + 1) * BS)
        g = part * chunk + j
        basis = right_ref[g, 0:BS]
        lg = right_ref[g, BS : BS + 16].astype(F32)[0:1]
        turned = dot(turned_left[...], grad_ref[:, cols], ((1,), (0,))).astype(BF16)
        rotated = dot(turned, basis, ((1,), (0,)))
        scaled = (rotated / (la * lg + DAMPING)).astype(BF16)
        returned = dot(scaled, basis, ((1,), (1,))).astype(BF16)
        out_ref[:, cols] = dot(left, returned, ((1,), (0,))).astype(BF16)
    block = block_ref[0, 0:BS]
    bases_ref[0] = jnp.where(used[slot] == 1, block, jnp.zeros_like(block))


def precondition(grad, blocks, left_index, la, right, place, used):
    rows, width = grad.shape[0] // BS, grad.shape[1] // BS
    cap = place.shape[0]
    chunk = next(c for c in (6, 4, 3, 2, 1) if width % c == 0 and rows * (width // c) >= cap)
    parts = width // chunk

    def slot(r, p):
        return jnp.minimum(r * parts + p, cap - 1)

    return pl.pallas_call(
        functools.partial(precondition_kernel, chunk),
        grid_spec=pltpu.PrefetchScalarGridSpec(
            num_scalar_prefetch=2,
            grid=(rows, parts),
            in_specs=[
                pl.BlockSpec((BS, chunk * BS), lambda r, p, at, u: (r, p)),
                pl.BlockSpec((1, ROWS, BS), lambda r, p, at, u: (left_index(r), 0, 0)),
                pl.BlockSpec((1, BS, 128), lambda r, p, at, u: (r, 0, 0)),
                pl.BlockSpec(right.shape, lambda r, p, at, u: (0, 0, 0)),
                pl.BlockSpec((1, ROWS, BS), lambda r, p, at, u: (at[slot(r, p)], 0, 0)),
            ],
            out_specs=[
                pl.BlockSpec((BS, chunk * BS), lambda r, p, at, u: (r, p)),
                pl.BlockSpec((1, BS, BS), lambda r, p, at, u: (slot(r, p), 0, 0)),
            ],
            scratch_shapes=[pltpu.VMEM((BS, BS), BF16)],
        ),
        out_shape=[
            jax.ShapeDtypeStruct(grad.shape, BF16),
            jax.ShapeDtypeStruct((cap, BS, BS), BF16),
        ],
        compiler_params=pltpu.CompilerParams(vmem_limit_bytes=48 * MIB),
        cost_estimate=pl.CostEstimate(
            flops=8 * BS**3 * rows * width, bytes_accessed=44 * MIB, transcendentals=0
        ),
        name="precondition",
    )(place, used, grad, blocks, la, right, blocks)


def shards(acts, out_grads, weight_grad, old_bases, owner_table):
    n, columns = lax.axis_size("dp"), lax.axis_size("owner")
    me = lax.axis_index("dp")
    blocks_a, blocks_g = acts.shape[1] // BS, out_grads.shape[1] // BS
    count = blocks_a + blocks_g
    cap = old_bases.shape[2]
    tokens = acts.shape[0] * n
    left, right = ceil_div(blocks_a, n), ceil_div(blocks_g, n)
    slots = left + right

    owners = owner_table[0, :, 0]
    order = jnp.arange(count, dtype=jnp.int32)
    same = owners[:, None] == owners[None, :]
    ranks = jnp.sum(jnp.where(same & (order[:, None] < order[None, :]), 1, 0), axis=0).astype(jnp.int32)

    is_left, block_a, block_g, block, real = [], [], [], [], []
    last_a, last_g = 0, 0
    for r in range(n):
        for s in range(slots):
            if s < left:
                b = r * left + s
                real.append(int(b < blocks_a))
                last_a = min(b, blocks_a - 1)
                is_left.append(1)
                block.append(last_a)
            else:
                b = r * right + s - left
                real.append(int(b < blocks_g))
                last_g = min(b, blocks_g - 1)
                is_left.append(0)
                block.append(blocks_a + last_g)
            block_a.append(last_a)
            block_g.append(last_g)
    as_int = functools.partial(jnp.array, dtype=jnp.int32)
    block_at = as_int(block)
    held = (jnp.take(owners, block_at) == me) & (as_int(real) == 1)
    old_slot = jnp.where(held, jnp.take(ranks, block_at), 0).astype(jnp.int32)

    mom, old = moments(
        acts, out_grads, old_bases[0, 0],
        as_int(is_left), as_int(block_a), as_int(block_g), old_slot, held.astype(jnp.int32),
    )
    shape = (n, slots, BS, BS)
    mom, old = reduce_blocks(n, slots, mom.reshape(shape), old.reshape(shape))
    fresh = refresh(mom, old, tokens)
    blocks, rights = spread(n, columns, left, fresh)
    blocks = blocks.reshape(n * slots, ROWS, BS)

    width = weight_grad.shape[1] // BS
    rights = rights.reshape(n * right, ROWS, BS)
    if n * right != width:
        rights = lax.dynamic_slice_in_dim(rights, me % (n // columns) * width, width, 0)

    def left_index(a):
        return a // left * slots + a % left

    values = blocks[:, BS]
    left_at = [left_index(a) for a in range(blocks_a)]
    la = jnp.concatenate([values[i : i + 1] for i in left_at]).astype(F32)
    la = jnp.broadcast_to(la[:, :, None], (blocks_a, BS, 128))

    places = as_int([left_index(a) for a in range(blocks_a)]
                    + [g // right * slots + left + g % right for g in range(blocks_g)])
    hit = (owners[None, :] == me) & (ranks[None, :] == jnp.arange(cap, dtype=jnp.int32)[:, None])
    place = jnp.sum(jnp.where(hit, places[None, :], 0), axis=1).astype(jnp.int32)
    used = jnp.any(hit, axis=1)
    chosen = (place[:, None] == jnp.arange(n * slots, dtype=jnp.int32)[None, :]) & used[:, None]
    new_values = jnp.dot(chosen.astype(BF16), values, preferred_element_type=F32).astype(BF16)

    result, new_bases = precondition(
        weight_grad, blocks, left_index, la, rights, place, used.astype(jnp.int32)
    )
    return (result, new_bases[None, None], new_values[None, None])


def solution(mesh):
    placed = (
        P(("groups", "dp"), "owner"),
        P(("groups", "dp"), "owner"),
        P(("groups", "owner"), "dp"),
        P(("groups", "owner"), "dp", None, None, None),
        P("owner", None, None),
    )
    return jax.shard_map(
        shards,
        mesh=mesh,
        in_specs=placed,
        out_specs=(
            P(("groups", "owner"), "dp"),
            P(("groups", "owner"), "dp", None, None, None),
            P(("groups", "owner"), "dp", None, None),
        ),
        check_vma=False,
    )
```

time: 494 us -> 272 us (0.55)
  Pallas kernels: 0 us -> 247 us
  matrix products: 200 us -> 0.79 us
  waiting for transfers between devices: 178 us -> 0 us
  local copies, waits for them, and re-layouts: 61.8 us -> 19.1 us
  blocking collectives: 24.9 us -> 0 us
  between operations: 14.3 us -> 0.74 us
  other arithmetic: 8.8 us -> 3.05 us
    pallas_call x0 -> x5, Pallas kernels: none -> 247 us  [the longest x1 90.8 us: spread(): pl.pallas_call(functools.partial(spread_kernel, n, columns, left), out_sh...]
    dot_general x26 -> x1, matrix products: 200 us -> 0.79 us  [shards(): jnp.dot(chosen.astype(BF16), values, preferred_element_type=F32)]
    psum x1 -> x0, waiting for transfers between devices: 81.4 us -> none  [from_root(): return lax.psum(kept, axis)]
    reduce_scatter x1 -> x0, waiting for transfers between devices: 74.3 us -> none  [shards(): lax.psum_scatter(outgoing, 'dp', scatter_dimension=0, tiled=True)]
    unnamed x13 -> x26, local copies, waits for them, and re-layouts: 42.5 us -> 15.1 us
    all_gather x1 -> x0, waiting for transfers between devices: 22.1 us -> none  [shards(): lax.all_gather(refreshed, 'dp', axis=0, tiled=True)]
    psum x1 -> x0, blocking collectives: 19.6 us -> none  [from_root(): return lax.psum(kept, axis)]
    convert_element_type x1 -> x0, local copies, waits for them, and re-layouts: 17.9 us -> none  [shards(): result = jnp.einsum('aik,akgj->aigj', left_basis, returned, preferred_ele...]
  transfers between devices with their start and end apart: 3 -> 0, of which waited for: 3 -> 0; matrix products, arithmetic and copies ran while one was open for 11% -> 0% of each run, Pallas kernels for 0% -> 0%
where the time goes in v1:
time: 272 us; the launch traced here: 270 us
  Pallas kernels  247 us (91%)
  local copies, waits for them, and re-layouts  19.1 us (7%)
  other arithmetic  3.05 us (1%)
    pallas_call x1, Pallas kernels, spread(): pl.pallas_call(functools.partial(spread_kernel, n, columns, left), out_sh...  90.8 us
    pallas_call x1, Pallas kernels, precondition(): pl.pallas_call(functools.partial(precondition_kernel, chunk), grid_spec=p...  65.2 us
    pallas_call x1, Pallas kernels, reduce_blocks(): pl.pallas_call(functools.partial(reduce_kernel, n, slots), out_shape=[jax...  57.3 us
    pallas_call x1, Pallas kernels, moments(): pl.pallas_call(kernel, grid_spec=pltpu.PrefetchScalarGridSpec(num_scalar_...  22.5 us
    unnamed x26, local copies, waits for them, and re-layouts  15.1 us
    pallas_call x1, Pallas kernels, refresh(): pl.pallas_call(functools.partial(refresh_kernel, group, tokens), grid=(sl...  11.1 us

profile of v1, /device:TPU:0, one launch (start us, length us, event | category | flops | bytes accessed | tf_op | source)
XLA Modules:
  0.0 270.5 jit_solution(6977552276178552872)
XLA Ops:
  0.6 0.8 select_reduce_fusion
  1.4 0.7 pad_clamp_fusion
  2.1 0.7 gather_fusion.1
  2.8 1.4 gather_fusion
  4.2 0.7 broadcast_select_fusion.old_slot
  4.8 0.7 fusion.10.held
  5.5 1.9 copy-done.2
  7.4 1.6 copy-done.3
  9.0 0.7 copy-done.5
  9.6 0.7 copy-done.6
  10.3 0.7 copy-done.7
  10.9 22.5 %moments.1 = (bf16[32,256,256]{2,1,0:T(8,128)(2,1)S(1)}, bf16[32,256,256]{2,1,0:T(8,128)(2,1)S(1)}) custom-call(s32[32]{0:T(128)S(1)} %copy-done.5, s32[32]{0:T(128)S(1)} %copy-done.6, s32[32]{0:T(128)S(1)} %copy-done.7, s32[32]{0:T(128)S(1)} %broadcast_select_fusion.old_slot, s32[32]{0:T(128)S(1)} %fusion.10.held, bf16[1024,1536]{1,0:T(8,128)(2,1)S(1)} %copy-done.2, ...), custom_call_target="tpu_custom_call" | custom-call | flops 4294967296 | bytes 25165824 | tf_op jit(solution)/shard_map/moments/pallas_call | solution.py:51
  33.4 0.0 copy-start
  33.4 2.0 copy-done
  35.4 1.9 copy-done.1
  37.4 57.3 %reduce_blocks.1 = (f32[8,256,256]{2,1,0:T(8,128)}, bf16[8,256,256]{2,1,0:T(8,128)(2,1)}) custom-call(bf16[4,8,256,256]{3,2,1,0:T(8,128)(2,1)} %bitcast.25, bf16[4,8,256,256]{3,2,1,0:T(8,128)(2,1)} %bitcast.26), custom_call_target="tpu_custom_call" | custom-call | flops 10485760 | bytes 16777216 | tf_op jit(solution)/shard_map/reduce_blocks/pallas_call | solution.py:142
  94.7 0.0 copy-start.9
  94.7 1.6 copy-done.9
  96.3 1.2 copy-done.10
  97.5 11.1 %refresh.1.fresh = bf16[8,272,256]{2,1,0:T(8,128)(2,1)S(1)} custom-call(f32[8,256,256]{2,1,0:T(8,128)S(1)} %copy-done.9, bf16[8,256,256]{2,1,0:T(8,128)(2,1)S(1)} %copy-done.10), custom_call_target="tpu_custom_call" | custom-call | flops 4831838208 | bytes 8388608 | tf_op jit(solution)/shard_map/refresh/pallas_call | solution.py:189
  108.6 0.0 copy-start.4
  108.6 1.0 copy-done.4
  109.6 90.8 %spread.1 = (bf16[4,8,272,256]{3,2,1,0:T(8,128)(2,1)}, bf16[4,6,272,256]{3,2,1,0:T(8,128)(2,1)}) custom-call(bf16[8,272,256]{2,1,0:T(8,128)(2,1)} %copy-done.4), custom_call_target="tpu_custom_call" | custom-call | bytes 16777216 | tf_op jit(solution)/shard_map/spread/pallas_call | solution.py:352
  200.3 0.7 slice_bitcast_fusion
  201.1 0.3 broadcast_in_dim.55.la_ref
  201.4 0.0 copy-done.11
  201.4 0.1 fusion.5
  201.5 0.1 select_reduce_fusion.1.place
  201.7 1.9 copy-done.8
  203.6 65.2 %precondition.1 = (bf16[1536,6144]{1,0:T(8,128)(2,1)}, bf16[16,256,256]{2,1,0:T(8,128)(2,1)}) custom-call(s32[16]{0:T(128)S(1)} %select_reduce_fusion.1.place, s32[16]{0:T(128)S(1)} %convert_element_type.17.used, bf16[1536,6144]{1,0:T(8,128)(2,1)} %grad_ref.1, bf16[32,272,256]{2,1,0:T(8,128)(2,1)} %bitcast.32, f32[6,256,128]{2,1,0:T(8,128)S(1)} %broadcast_in_dim.55.la_ref, ...), custom_call_target="tpu_custom_call" | custom-call | flops 19327352832 | bytes 46137344 | tf_op jit(solution)/shard_map/precondition/pallas_call | solution.py:408
  268.8 0.9 slice.50
  269.7 0.8 fusion
  (14 shorter events, 0.1 us)
Async XLA Ops:
  5.5 1.9 copy-start.2
  7.4 1.6 copy-start.3
  9.0 0.7 copy-start.5
  9.6 0.7 copy-start.6
  10.3 0.7 copy-start.7
  33.4 2.0 copy-start
  35.4 1.9 copy-start.1
  94.7 1.6 copy-start.9
  96.3 1.2 copy-start.10
  97.5 103.9 %copy-start.11 = (s32[1,30,1]{1,2,0:T(1,128)S(1)}, s32[1,30,1]{1,2,0:T(1,128)}, u32[]{:S(2)}) copy-start(s32[1,30,1]{1,2,0:T(1,128)} %param.17) | copy-start | bytes 364
  97.5 104.0 %copy-start.12 = (s32[30]{0:T(128)S(1)}, s32[30]{0:T(128)}, u32[]{:S(2)}) copy-start(s32[30]{0:T(128)} %constant.39.clone) | copy-start | bytes 364
  108.6 1.0 copy-start.4
  201.7 1.9 copy-start.8

commit v2 on v1

v2 whole, which is shorter than its diff:
```python
import functools

import jax
import jax.numpy as jnp
from jax import lax
from jax.experimental import pallas as pl
from jax.experimental.pallas import tpu as pltpu
from jax.sharding import PartitionSpec as P

BS = 256
ROWS = BS + 16
ORTHO_STEPS = 8
DAMPING = 0.1
F32 = jnp.float32
BF16 = jnp.bfloat16
MIB = 1 << 20


def dot(a, b, contract):
    return lax.dot_general(a, b, (contract, ((), ())), preferred_element_type=F32)


def ceil_div(a, b):
    return -(-a // b)


def moments_kernel(left, right, acts_ref, grads_ref, out_ref):
    for s in range(left + right):
        ref, at = (acts_ref, s) if s < left else (grads_ref, s - left)
        x = ref[:, at * BS : (at + 1) * BS]
        out_ref[0, s] = dot(x, x, ((0,), (0,))).astype(BF16)


def moments(n, left, right, acts, grads):
    tokens = acts.shape[0]
    slots = left + right
    last_a = acts.shape[1] // (left * BS) - 1
    last_g = grads.shape[1] // (right * BS) - 1
    return pl.pallas_call(
        functools.partial(moments_kernel, left, right),
        grid=(n,),
        in_specs=[
            pl.BlockSpec((tokens, left * BS), lambda r: (0, jnp.minimum(r, last_a))),
            pl.BlockSpec((tokens, right * BS), lambda r: (0, jnp.minimum(r, last_g))),
        ],
        out_specs=pl.BlockSpec((1, slots, BS, BS), lambda r: (r, 0, 0, 0)),
        out_shape=jax.ShapeDtypeStruct((n, slots, BS, BS), BF16),
        compiler_params=pltpu.CompilerParams(vmem_limit_bytes=40 * MIB),
        cost_estimate=pl.CostEstimate(
            flops=2 * n * slots * tokens * BS * BS, bytes_accessed=20 * MIB, transcendentals=0
        ),
        name="moments",
    )(acts, grads)


def reduce_kernel(n, slots, mom, out, near, far, own, near_send, near_recv, far_send, far_recv):
    me = lax.axis_index("dp")
    pairs = n // 2
    chip, core = me // 2, lax.rem(me, 2)
    partner = chip * 2 + (1 - core)
    half = slots // 2
    pieces = [(0, half), (half, slots)]

    barrier = pltpu.get_barrier_semaphore()
    pl.semaphore_signal(barrier, inc=1, device_id={"dp": partner})
    for k in range(1, pairs):
        there = lax.rem(chip + k, pairs) * 2 + core
        pl.semaphore_signal(barrier, inc=1, device_id={"dp": there})
    pl.semaphore_wait(barrier, pairs)

    def to_partner(k, part):
        target = lax.rem(chip + k, pairs) * 2 + (1 - core)
        some = pl.ds(pieces[part][0], pieces[part][1] - pieces[part][0])
        return pltpu.make_async_remote_copy(
            src_ref=mom.at[target, some],
            dst_ref=near.at[k - 1, some],
            send_sem=near_send.at[k - 1, part],
            recv_sem=near_recv.at[k - 1, part],
            device_id={"dp": partner},
        )

    def to_chip(k, part):
        some = pl.ds(pieces[part][0], pieces[part][1] - pieces[part][0])
        return pltpu.make_async_remote_copy(
            src_ref=own.at[k - 1, some],
            dst_ref=far.at[k - 1, some],
            send_sem=far_send.at[k - 1, part],
            recv_sem=far_recv.at[k - 1, part],
            device_id={"dp": lax.rem(chip + k, pairs) * 2 + core},
        )

    order = [(k, part) for k in range(1, pairs + 1) for part in (0, 1)]
    for k, part in order:
        to_partner(k, part).start()
    for k, part in order:
        to_partner(k, part).wait()
        mine = lax.rem(chip + k, pairs) * 2 + core

        @pl.loop(*pieces[part])
        def _(s):
            own[k - 1, s] = (mom[mine, s].astype(F32) + near[k - 1, s].astype(F32)).astype(BF16)

        if k < pairs:
            to_chip(k, part).start()
    for part in (0, 1):
        for k in range(1, pairs):
            to_chip(k, part).wait()

        @pl.loop(*pieces[part])
        def _(s):
            total = own[pairs - 1, s].astype(F32)
            for k in range(1, pairs):
                total = total + far[k - 1, s].astype(F32)
            out[s] = total


def reduce_blocks(n, slots, mom):
    pairs = n // 2
    vmem = pl.BlockSpec(memory_space=pltpu.VMEM)
    buffer = pltpu.VMEM((pairs, slots, BS, BS), BF16)
    return pl.pallas_call(
        functools.partial(reduce_kernel, n, slots),
        out_shape=jax.ShapeDtypeStruct((slots, BS, BS), F32),
        in_specs=[vmem],
        out_specs=vmem,
        scratch_shapes=[buffer] * 3 + [pltpu.SemaphoreType.DMA((pairs, 2))] * 4,
        compiler_params=pltpu.CompilerParams(
            collective_id=0, has_side_effects=True, vmem_limit_bytes=40 * MIB
        ),
        cost_estimate=pl.CostEstimate(flops=10 * MIB, bytes_accessed=16 * MIB, transcendentals=0),
        name="reduce_blocks",
    )(mom)


def refresh_kernel(group, tokens, at, mom_ref, *refs):
    old_refs, (out_ref, current) = refs[:group], refs[group:]
    for s in range(group):
        moment = mom_ref[s] * (1.0 / tokens)
        product = dot(moment.astype(BF16), old_refs[s][0], ((1,), (0,)))
        current[s] = product / jnp.sqrt(jnp.sum(product * product) + 1e-06)

    @pl.loop(0, ORTHO_STEPS)
    def _(step):
        rounded = [current[s].astype(BF16) for s in range(group)]
        grams = [dot(y, y, ((0,), (0,))).astype(BF16) for y in rounded]
        for s in range(group):
            current[s] = 1.5 * current[s] - 0.5 * dot(rounded[s], grams[s], ((1,), (0,)))

    for s in range(group):
        moment = mom_ref[s] * (1.0 / tokens)
        high = moment.astype(BF16)
        low = (moment - high.astype(F32)).astype(BF16)
        y = current[s]
        basis = y.astype(BF16)
        applied = dot(high, basis, ((1,), (0,))) + dot(low, basis, ((1,), (0,)))
        top = jnp.mean(applied * y, axis=0, keepdims=True)
        value = top / (jnp.mean(y * y, axis=0, keepdims=True) + 1e-06)
        out_ref[s, 0:BS] = basis
        out_ref[s, BS:ROWS] = jnp.broadcast_to(value, (ROWS - BS, BS)).astype(BF16)


def refresh(mom, old, at, tokens):
    slots = mom.shape[0]
    group = 4 if slots % 4 == 0 else (2 if slots % 2 == 0 else 1)

    def previous(j):
        return pl.BlockSpec((1, BS, BS), lambda i, at: (at[i * group + j], 0, 0))

    return pl.pallas_call(
        functools.partial(refresh_kernel, group, tokens),
        grid_spec=pltpu.PrefetchScalarGridSpec(
            num_scalar_prefetch=1,
            grid=(slots // group,),
            in_specs=[pl.BlockSpec((group, BS, BS), lambda i, at: (i, 0, 0))]
            + [previous(j) for j in range(group)],
            out_specs=pl.BlockSpec((group, ROWS, BS), lambda i, at: (i, 0, 0)),
            scratch_shapes=[pltpu.VMEM((group, BS, BS), F32)],
        ),
        out_shape=jax.ShapeDtypeStruct((slots, ROWS, BS), BF16),
        compiler_params=pltpu.CompilerParams(vmem_limit_bytes=32 * MIB),
        cost_estimate=pl.CostEstimate(
            flops=36 * slots * BS**3, bytes_accessed=8 * MIB, transcendentals=0
        ),
        name="refresh",
    )(at, mom, *([old] * group))


def spread_kernel(
    n, columns, left, fresh, column_blocks, right, held, up_send, up_recv, down_send, down_recv,
    give_send, give_recv, chip_send, chip_recv, core_send, core_recv, local_sem,
):
    me, here = lax.axis_index("dp"), lax.axis_index("owner")
    per = n // columns
    above = jnp.minimum(here + 1, columns - 1)
    below = jnp.maximum(here - 1, 0)
    has_above, has_below = here < columns - 1, here > 0

    barrier = pltpu.get_barrier_semaphore()
    for k in range(1, n):
        pl.semaphore_signal(barrier, inc=1, device_id={"dp": lax.rem(me + k, n)})

    @pl.when(has_above)
    def _():
        pl.semaphore_signal(barrier, inc=1, device_id={"owner": above})

    @pl.when(has_below)
    def _():
        pl.semaphore_signal(barrier, inc=1, device_id={"owner": below})

    pl.semaphore_wait(barrier, n - 1 + jnp.where(has_above, 1, 0) + jnp.where(has_below, 1, 0))

    held[here] = fresh[left:]

    def along(k, column, send, recv, there):
        return pltpu.make_async_remote_copy(
            src_ref=held.at[column],
            dst_ref=held.at[column],
            send_sem=send.at[k],
            recv_sem=recv.at[k],
            device_id={"owner": there},
        )

    def clamp(column):
        return jnp.clip(column, 0, columns - 1)

    def up(k, column):
        return along(k, clamp(column), up_send, up_recv, above)

    def down(k, column):
        return along(k, clamp(column), down_send, down_recv, below)

    def give(column, target):
        return pltpu.make_async_remote_copy(
            src_ref=held.at[column],
            dst_ref=right.at[me],
            send_sem=give_send.at[target],
            recv_sem=give_recv.at[me],
            device_id={"dp": target},
        )

    def taken(source):
        return pltpu.make_async_remote_copy(
            src_ref=held.at[0],
            dst_ref=right.at[source],
            send_sem=give_send.at[source],
            recv_sem=give_recv.at[source],
            device_id={"dp": source},
        )

    def keep(column):
        return pltpu.make_async_copy(held.at[column], right.at[me], local_sem.at[0])

    def share(column):
        for h in range(per):
            target = column * per + h

            @pl.when(target != me)
            def _():
                give(column, target).start()

            @pl.when(target == me)
            def _():
                keep(column).start()

    pairs = n // 2
    chip, core = me // 2, lax.rem(me, 2)
    partner = chip * 2 + (1 - core)

    def to_chip(k):
        return pltpu.make_async_remote_copy(
            src_ref=fresh,
            dst_ref=column_blocks.at[me],
            send_sem=chip_send.at[k - 1],
            recv_sem=chip_recv.at[k - 1],
            device_id={"dp": lax.rem(chip + k, pairs) * 2 + core},
        )

    def source(k):
        return lax.rem(chip + pairs - k, pairs) * 2 + core

    def to_partner(k):
        return pltpu.make_async_remote_copy(
            src_ref=fresh if k == 0 else column_blocks.at[source(k)],
            dst_ref=column_blocks.at[source(k)],
            send_sem=core_send.at[k],
            recv_sem=core_recv.at[k],
            device_id={"dp": partner},
        )

    mine = pltpu.make_async_copy(fresh, column_blocks.at[me], local_sem.at[1])
    for k in range(columns - 1):
        sends_up = has_above & (here - k >= 0)
        sends_down = has_below & (here + k <= columns - 1)

        @pl.when(sends_up)
        def _():
            up(k, here - k).start()

        @pl.when(sends_down)
        def _():
            down(k, here + k).start()

        if k == 0:
            share(here)
            mine.start()
            for j in range(1, pairs):
                to_chip(j).start()
            to_partner(0).start()

        if k == 1:
            for j in range(1, pairs):
                to_chip(j).wait_recv()
                to_partner(j).start()

        @pl.when(here - 1 - k >= 0)
        def _():
            up(k, here - 1 - k).wait_recv()
            share(clamp(here - 1 - k))

        @pl.when(here + 1 + k <= columns - 1)
        def _():
            down(k, here + 1 + k).wait_recv()
            share(clamp(here + 1 + k))

    for k in range(columns - 1):

        @pl.when(has_above & (here - k >= 0))
        def _():
            up(k, here - k).wait_send()

        @pl.when(has_below & (here + k <= columns - 1))
        def _():
            down(k, here + k).wait_send()

    mine.wait()
    keep(here).wait()
    for k in range(pairs):
        to_partner(k).wait()
        if k > 0:
            to_chip(k).wait_send()
    for k in range(1, n):
        other = lax.rem(me + k, n)
        taken(other).wait_send()
        taken(other).wait_recv()


def spread(n, columns, left, fresh):
    slots = fresh.shape[0]
    dma = pltpu.SemaphoreType.DMA
    vmem = pl.BlockSpec(memory_space=pltpu.VMEM)
    return pl.pallas_call(
        functools.partial(spread_kernel, n, columns, left),
        out_shape=[
            jax.ShapeDtypeStruct((n, slots, ROWS, BS), BF16),
            jax.ShapeDtypeStruct((n, slots - left, ROWS, BS), BF16),
        ],
        in_specs=[vmem],
        out_specs=[vmem, vmem],
        scratch_shapes=[pltpu.VMEM((columns, slots - left, ROWS, BS), BF16)]
        + [dma((columns - 1,))] * 4
        + [dma((n,))] * 2
        + [dma((max(1, n // 2 - 1),))] * 2
        + [dma((n // 2,))] * 2
        + [dma((2,))],
        compiler_params=pltpu.CompilerParams(
            collective_id=1, has_side_effects=True, vmem_limit_bytes=56 * MIB
        ),
        cost_estimate=pl.CostEstimate(flops=0, bytes_accessed=16 * MIB, transcendentals=0),
        name="spread",
    )(fresh)


def precondition_kernel(
    rows, place, used, grad_ref, left_ref, turned_left_ref, la_ref, right_ref, block_ref, out_ref, bases_ref,
):
    slot = jnp.minimum(pl.program_id(0), used.shape[0] - 1)
    basis = right_ref[0, 0:BS]
    lg = right_ref[0, BS:ROWS].astype(F32)[0:1]
    turned = [
        dot(turned_left_ref[a], grad_ref[a * BS : (a + 1) * BS], ((1,), (0,))).astype(BF16)
        for a in range(rows)
    ]
    rotated = [dot(turned[a], basis, ((1,), (0,))) for a in range(rows)]
    scaled = [
        (rotated[a] / (la_ref[a][:, 0:1] * lg + DAMPING)).astype(BF16) for a in range(rows)
    ]
    returned = [dot(scaled[a], basis, ((1,), (1,))).astype(BF16) for a in range(rows)]
    for a in range(rows):
        out_ref[a * BS : (a + 1) * BS] = dot(left_ref[a], returned[a], ((1,), (0,))).astype(BF16)
    block = block_ref[0, 0:BS]
    bases_ref[0] = jnp.where(used[slot] == 1, block, jnp.zeros_like(block))


def precondition(grad, left, turned_left, la, right, blocks, place, used):
    rows, width = grad.shape[0] // BS, grad.shape[1] // BS
    cap = place.shape[0]
    assert width >= cap

    def slot(g):
        return jnp.minimum(g, cap - 1)

    def whole(g, at, u):
        return (0, 0, 0)

    return pl.pallas_call(
        functools.partial(precondition_kernel, rows),
        grid_spec=pltpu.PrefetchScalarGridSpec(
            num_scalar_prefetch=2,
            grid=(width,),
            in_specs=[
                pl.BlockSpec((rows * BS, BS), lambda g, at, u: (0, g)),
                pl.BlockSpec((rows, BS, BS), whole),
                pl.BlockSpec((rows, BS, BS), whole),
                pl.BlockSpec((rows, BS, 128), whole),
                pl.BlockSpec((1, ROWS, BS), lambda g, at, u: (g, 0, 0)),
                pl.BlockSpec((1, ROWS, BS), lambda g, at, u: (at[slot(g)], 0, 0)),
            ],
            out_specs=[
                pl.BlockSpec((rows * BS, BS), lambda g, at, u: (0, g)),
                pl.BlockSpec((1, BS, BS), lambda g, at, u: (slot(g), 0, 0)),
            ],
        ),
        out_shape=[
            jax.ShapeDtypeStruct(grad.shape, BF16),
            jax.ShapeDtypeStruct((cap, BS, BS), BF16),
        ],
        compiler_params=pltpu.CompilerParams(vmem_limit_bytes=48 * MIB),
        cost_estimate=pl.CostEstimate(
            flops=8 * BS**3 * rows * width, bytes_accessed=44 * MIB, transcendentals=0
        ),
        name="precondition",
    )(place, used, grad, left, turned_left, la, right, blocks)


def shards(acts, out_grads, weight_grad, old_bases, owner_table):
    n, columns = lax.axis_size("dp"), lax.axis_size("owner")
    me = lax.axis_index("dp")
    blocks_a, blocks_g = acts.shape[1] // BS, out_grads.shape[1] // BS
    count = blocks_a + blocks_g
    cap = old_bases.shape[2]
    tokens = acts.shape[0] * n
    left, right = ceil_div(blocks_a, n), ceil_div(blocks_g, n)
    slots = left + right

    owners = owner_table[0, :, 0]
    order = jnp.arange(count, dtype=jnp.int32)
    same = owners[:, None] == owners[None, :]
    ranks = jnp.sum(jnp.where(same & (order[:, None] < order[None, :]), 1, 0), axis=0).astype(jnp.int32)

    def left_index(a):
        return a // left * slots + a % left

    as_int = functools.partial(jnp.array, dtype=jnp.int32)
    places = as_int([left_index(a) for a in range(blocks_a)]
                    + [g // right * slots + left + g % right for g in range(blocks_g)])
    here = places[None, :] == (me * slots + jnp.arange(slots, dtype=jnp.int32))[:, None]
    old_at = jnp.sum(jnp.where(here, (owners * cap + ranks)[None, :], 0), axis=1).astype(jnp.int32)

    old = lax.all_gather(old_bases[0, 0], "dp", axis=0, tiled=True)
    mom = reduce_blocks(n, slots, moments(n, left, right, acts, out_grads))
    fresh = refresh(mom, old, old_at, tokens)
    blocks, rights = spread(n, columns, left, fresh)
    blocks = blocks.reshape(n * slots, ROWS, BS)

    width = weight_grad.shape[1] // BS
    rights = rights.reshape(n * right, ROWS, BS)
    if n * right != width:
        rights = lax.dynamic_slice_in_dim(rights, me % (n // columns) * width, width, 0)

    left_at = [left_index(a) for a in range(blocks_a)]
    left_basis = jnp.stack([blocks[i, 0:BS] for i in left_at])
    turned_left = jnp.swapaxes(left_basis, 1, 2)
    values = blocks[:, BS]
    la = jnp.stack([values[i] for i in left_at]).astype(F32)
    la = jnp.broadcast_to(la[:, :, None], (blocks_a, BS, 128))

    hit = (owners[None, :] == me) & (ranks[None, :] == jnp.arange(cap, dtype=jnp.int32)[:, None])
    place = jnp.sum(jnp.where(hit, places[None, :], 0), axis=1).astype(jnp.int32)
    used = jnp.any(hit, axis=1)
    chosen = (place[:, None] == jnp.arange(n * slots, dtype=jnp.int32)[None, :]) & used[:, None]
    new_values = jnp.dot(chosen.astype(BF16), values, preferred_element_type=F32).astype(BF16)

    result, new_bases = precondition(
        weight_grad, left_basis, turned_left, la, rights, blocks, place, used.astype(jnp.int32)
    )
    return (result, new_bases[None, None], new_values[None, None])


def solution(mesh):
    placed = (
        P(("groups", "dp"), "owner"),
        P(("groups", "dp"), "owner"),
        P(("groups", "owner"), "dp"),
        P(("groups", "owner"), "dp", None, None, None),
        P("owner", None, None),
    )
    return jax.shard_map(
        shards,
        mesh=mesh,
        in_specs=placed,
        out_specs=(
            P(("groups", "owner"), "dp"),
            P(("groups", "owner"), "dp", None, None, None),
            P(("groups", "owner"), "dp", None, None),
        ),
        check_vma=False,
    )
```

time: 272 us -> 243 us (0.89)
  Pallas kernels: 247 us -> 191 us
  waiting for transfers between devices: 0 us -> 21.8 us
  between operations: 0.74 us -> 14.2 us
  local copies, waits for them, and re-layouts: 19.1 us -> 11.6 us
    pallas_call x4, Pallas kernels: 156 us -> 105 us  [the longest x1 52.2 us: reduce_blocks(): pl.pallas_call(functools.partial(reduce_kernel, n, slots), out_shape=jax....]
    all_gather x0 -> x1, waiting for transfers between devices: none -> 21.1 us  [shards(): old = lax.all_gather(old_bases[0, 0], 'dp', axis=0, tiled=True)]
    unnamed x26 -> x12, local copies, waits for them, and re-layouts: 15.1 us -> 8.21 us
    pallas_call x1, Pallas kernels: 90.8 us -> 86.1 us  [spread(): pl.pallas_call(functools.partial(spread_kernel, n, columns, left), out_sh...]
  transfers between devices with their start and end apart: 0 -> 1, of which waited for: 0 -> 1; matrix products, arithmetic and copies ran while one was open for 0% -> 1% of each run, Pallas kernels for 0% -> 25%
where the time goes in v2:
time: 243 us; the launch traced here: 241 us
  Pallas kernels  191 us (79%)
  waiting for transfers between devices  21.8 us (9%)
  between operations  14.2 us (6%)
  local copies, waits for them, and re-layouts  11.6 us (5%)
    pallas_call x1, Pallas kernels, spread(): pl.pallas_call(functools.partial(spread_kernel, n, columns, left), out_sh...  86.1 us
    pallas_call x1, Pallas kernels, reduce_blocks(): pl.pallas_call(functools.partial(reduce_kernel, n, slots), out_shape=jax....  52.2 us
    pallas_call x1, Pallas kernels, precondition(): pl.pallas_call(functools.partial(precondition_kernel, rows), grid_spec=pl...  33.1 us
    all_gather x1, waiting for transfers between devices, shards(): old = lax.all_gather(old_bases[0, 0], 'dp', axis=0, tiled=True)  21.1 us
    pallas_call x1, Pallas kernels, refresh(): pl.pallas_call(functools.partial(refresh_kernel, group, tokens), grid_spe...  11.6 us
    unnamed x12, local copies, waits for them, and re-layouts  8.21 us
    pallas_call x1, Pallas kernels, moments(): pl.pallas_call(functools.partial(moments_kernel, left, right), grid=(n,),...  8.04 us
  transfers between devices with their start and end apart: 1, of which 1 were waited for; matrix products, arithmetic and copies ran while one was open for 1% of the time, Pallas kernels for 25%

profile of v2, /device:TPU:0, one launch (start us, length us, event | category | flops | bytes accessed | tf_op | source)
XLA Modules:
  0.0 241.3 jit_solution(2831230193608506804)
XLA Ops:
  7.2 0.0 all-gather.3.cloned.1.call-start
  7.2 0.7 all-gather.3.cloned.1.call-update
  7.9 0.8 select_reduce_fusion
  8.7 0.7 broadcast_compare_fusion
  9.4 0.1 fusion.5
  9.5 0.0 copy-start.2
  9.5 1.9 copy-done.2
  11.4 8.0 %moments.1.mom = bf16[4,8,256,256]{3,2,1,0:T(8,128)(2,1)S(1)} custom-call(bf16[1024,1536]{1,0:T(8,128)(2,1)S(1)} %copy-done.2, bf16[1024,6144]{1,0:T(8,128)(2,1)} %grads_ref.1), custom_call_target="tpu_custom_call" | custom-call | flops 4294967296 | bytes 20971520 | tf_op jit(solution)/shard_map/moments/pallas_call | solution.py:39
  19.4 0.0 copy-start.4
  19.5 0.0 copy-start.5
  19.5 52.2 %reduce_blocks.1.mom_ref = f32[8,256,256]{2,1,0:T(8,128)S(1)} custom-call(bf16[4,8,256,256]{3,2,1,0:T(8,128)(2,1)S(1)} %moments.1.mom), custom_call_target="tpu_custom_call" | custom-call | flops 10485760 | bytes 16777216 | tf_op jit(solution)/shard_map/reduce_blocks/pallas_call | solution.py:121
  71.6 0.0 copy-done.4
  71.7 0.1 select_reduce_fusion.1.place
  71.8 0.0 copy-done.5
  71.8 0.2 select_reduce_fusion.2.at
  72.0 21.1 %all-gather.3.cloned.1.call-done = bf16[1,1,64,256,256]{4,3,1,0,2:T(8,128)(2,1)} async-done(((bf16[1,1,16,256,256]{4,3,1,0,2:T(8,128)(2,1)}), bf16[1,1,64,256,256]{4,3,1,0,2:T(8,128)(2,1)}) %all-gather.3.cloned.1.call-update) | async-done | bytes 8388624 | tf_op jit(solution)/shard_map/all_gather | solution.py:459
  93.0 0.0 copy-start
  93.0 3.4 %copy-done = bf16[1,1,64,256,256]{4,3,1,0,2:T(8,128)(2,1)S(1)} copy-done((bf16[1,1,64,256,256]{4,3,1,0,2:T(8,128)(2,1)S(1)}, bf16[1,1,64,256,256]{4,3,1,0,2:T(8,128)(2,1)}, u32[]{:S(2)}) %copy-start) | copy-done | bytes 8388632
  96.4 11.6 %refresh.1.fresh = bf16[8,272,256]{2,1,0:T(8,128)(2,1)S(1)} custom-call(s32[8]{0:T(128)S(1)} %select_reduce_fusion.2.at, f32[8,256,256]{2,1,0:T(8,128)S(1)} %reduce_blocks.1.mom_ref, bf16[64,256,256]{2,1,0:T(8,128)(2,1)S(1)} %bitcast.27, bf16[64,256,256]{2,1,0:T(8,128)(2,1)S(1)} %bitcast.28, bf16[64,256,256]{2,1,0:T(8,128)(2,1)S(1)} %bitcast.29, ...), custom_call_target="tpu_custom_call" | custom-call | flops 4831838208 | bytes 8388608 | tf_op jit(solution)/shard_map/refresh/pallas_call | solution.py:169
  108.0 0.0 copy-start.1
  108.1 1.0 copy-done.1
  109.0 86.1 %spread.1 = (bf16[4,8,272,256]{3,2,1,0:T(8,128)(2,1)}, bf16[4,6,272,256]{3,2,1,0:T(8,128)(2,1)}) custom-call(bf16[8,272,256]{2,1,0:T(8,128)(2,1)} %copy-done.1), custom_call_target="tpu_custom_call" | custom-call | bytes 16777216 | tf_op jit(solution)/shard_map/spread/pallas_call | solution.py:351
  195.1 0.7 slice_bitcast_fusion
  195.9 1.2 fusion.11
  197.0 0.9 slice.67
  198.0 0.1 fusion.10
  198.1 0.3 copy.14.turned_left_ref
  198.4 0.8 fusion
  199.2 0.3 broadcast_in_dim.61.la_ref
  199.4 0.0 copy-start.3
  199.4 1.9 copy-done.3
  201.4 33.1 %precondition.1 = (bf16[1536,6144]{1,0:T(8,128)(2,1)}, bf16[16,256,256]{2,1,0:T(8,128)(2,1)}) custom-call(s32[16]{0:T(128)S(1)} %select_reduce_fusion.1.place, s32[16]{0:T(128)S(1)} %convert_element_type.14.used, bf16[1536,6144]{1,0:T(8,128)(2,1)} %grad_ref.1, bf16[6,256,256]{2,1,0:T(8,128)(2,1)S(1)} %get-tuple-element.21.left_ref, ...), custom_call_target="tpu_custom_call" | custom-call | flops 19327352832 | bytes 46137344 | tf_op jit(solution)/shard_map/precondition/pallas_call | solution.py:405
  (4 shorter events, 0.0 us)
Async XLA Ops:
  7.2 85.9 %all-gather.3.cloned.1.call-start = ((), (), s32[]{:S(2)}) async-start(), calls=%async_computation | async-start | bytes 10485760 | tf_op jit(solution)/shard_map/all_gather | solution.py:459
  9.5 1.9 copy-start.2
  19.4 52.2 %copy-start.4 = (s32[30]{0:T(128)S(1)}, s32[30]{0:T(128)}, u32[]{:S(2)}) copy-start(s32[30]{0:T(128)} %constant.17.clone) | copy-start | bytes 364
  19.5 52.3 %copy-start.5 = (s32[1,30,1]{1,2,0:T(1,128)S(1)}, s32[1,30,1]{1,2,0:T(1,128)}, u32[]{:S(2)}) copy-start(s32[1,30,1]{1,2,0:T(1,128)} %param.10) | copy-start | bytes 364
  93.0 3.4 %copy-start = (bf16[1,1,64,256,256]{4,3,1,0,2:T(8,128)(2,1)S(1)}, bf16[1,1,64,256,256]{4,3,1,0,2:T(8,128)(2,1)}, u32[]{:S(2)}) copy-start(bf16[1,1,64,256,256]{4,3,1,0,2:T(8,128)(2,1)} %all-gather.3.cloned.1.call-done) | copy-start | bytes 25165828
  108.0 1.0 copy-start.1
  199.4 2.0 copy-start.3
Sparse Core Ops, SparseCore 0:
  9.6 83.4 all-gather.2

commit v3 on v2

--- a/solution.py
+++ b/solution.py
@@ -24,42 +24,45 @@
     return -(-a // b)
 
 
-def moments_kernel(left, right, acts_ref, grads_ref, out_ref):
-    for s in range(left + right):
-        ref, at = (acts_ref, s) if s < left else (grads_ref, s - left)
-        x = ref[:, at * BS : (at + 1) * BS]
-        out_ref[0, s] = dot(x, x, ((0,), (0,))).astype(BF16)
-
-
-def moments(n, left, right, acts, grads):
-    tokens = acts.shape[0]
+def arrange_kernel(each, at, held, *refs):
+    out_ref = refs[each]
+    for j in range(each):
+        old = refs[j][0]
+        out_ref[j] = jnp.where(held[pl.program_id(0) * each + j] == 1, old, jnp.zeros_like(old))
+
+
+def arrange(old, at, held):
+    count = at.shape[0]
+    each = 8 if count % 8 == 0 else 1
+
+    def one(j):
+        return pl.BlockSpec((1, BS, BS), lambda i, at, h: (at[i * each + j], 0, 0))
+
+    return pl.pallas_call(
+        functools.partial(arrange_kernel, each),
+        grid_spec=pltpu.PrefetchScalarGridSpec(
+            num_scalar_prefetch=2,
+            grid=(count // each,),
+            in_specs=[one(j) for j in range(each)],
+            out_specs=pl.BlockSpec((each, BS, BS), lambda i, at, h: (i, 0, 0)),
+        ),
+        out_shape=jax.ShapeDtypeStruct((count, BS, BS), BF16),
+        compiler_params=pltpu.CompilerParams(vmem_limit_bytes=16 * MIB),
+        cost_estimate=pl.CostEstimate(flops=0, bytes_accessed=8 * MIB, transcendentals=0),
+        name="arrange",
+    )(at, held, *([old] * each))
+
+
+def reduce_kernel(
+    n, left, right, acts, grads, old, mom_out, old_out, mom, near, far, own, near_send, near_recv, far_send, far_recv,
+):
     slots = left + right
     last_a = acts.shape[1] // (left * BS) - 1
     last_g = grads.shape[1] // (right * BS) - 1
-    return pl.pallas_call(
-        functools.partial(moments_kernel, left, right),
-        grid=(n,),
-        in_specs=[
-            pl.BlockSpec((tokens, left * BS), lambda r: (0, jnp.minimum(r, last_a))),
-            pl.BlockSpec((tokens, right * BS), lambda r: (0, jnp.minimum(r, last_g))),
-        ],
-        out_specs=pl.BlockSpec((1, slots, BS, BS), lambda r: (r, 0, 0, 0)),
-        out_shape=jax.ShapeDtypeStruct((n, slots, BS, BS), BF16),
-        compiler_params=pltpu.CompilerParams(vmem_limit_bytes=40 * MIB),
-        cost_estimate=pl.CostEstimate(
-            flops=2 * n * slots * tokens * BS * BS, bytes_accessed=20 * MIB, transcendentals=0
-        ),
-        name="moments",
-    )(acts, grads)
-
-
-def reduce_kernel(n, slots, mom, out, near, far, own, near_send, near_recv, far_send, far_recv):
     me = lax.axis_index("dp")
     pairs = n // 2
     chip, core = me // 2, lax.rem(me, 2)
     partner = chip * 2 + (1 - core)
-    half = slots // 2
-    pieces = [(0, half), (half, slots)]
 
     barrier = pltpu.get_barrier_semaphore()
     pl.semaphore_signal(barrier, inc=1, device_id={"dp": partner})
@@ -70,73 +73,98 @@
 
     def to_partner(k, part):
         target = lax.rem(chip + k, pairs) * 2 + (1 - core)
-        some = pl.ds(pieces[part][0], pieces[part][1] - pieces[part][0])
-        return pltpu.make_async_remote_copy(
-            src_ref=mom.at[target, some],
-            dst_ref=near.at[k - 1, some],
+        return pltpu.make_async_remote_copy(
+            src_ref=(old, mom)[part].at[target],
+            dst_ref=near.at[k - 1, part],
             send_sem=near_send.at[k - 1, part],
             recv_sem=near_recv.at[k - 1, part],
             device_id={"dp": partner},
         )
 
     def to_chip(k, part):
-        some = pl.ds(pieces[part][0], pieces[part][1] - pieces[part][0])
-        return pltpu.make_async_remote_copy(
-            src_ref=own.at[k - 1, some],
-            dst_ref=far.at[k - 1, some],
+        return pltpu.make_async_remote_copy(
+            src_ref=own.at[k - 1, part],
+            dst_ref=far.at[k - 1, part],
             send_sem=far_send.at[k - 1, part],
             recv_sem=far_recv.at[k - 1, part],
             device_id={"dp": lax.rem(chip + k, pairs) * 2 + core},
         )
 
-    order = [(k, part) for k in range(1, pairs + 1) for part in (0, 1)]
-    for k, part in order:
-        to_partner(k, part).start()
-    for k, part in order:
-        to_partner(k, part).wait()
-        mine = lax.rem(chip + k, pairs) * 2 + core
-
-        @pl.loop(*pieces[part])
-        def _(s):
-            own[k - 1, s] = (mom[mine, s].astype(F32) + near[k - 1, s].astype(F32)).astype(BF16)
-
-        if k < pairs:
-            to_chip(k, part).start()
+    def moments():
+        @pl.loop(0, n)
+        def _(r):
+            for s in range(slots):
+                if s < left:
+                    ref, at = acts, (jnp.minimum(r, last_a) * left + s) * BS
+                else:
+                    ref, at = grads, (jnp.minimum(r, last_g) * right + s - left) * BS
+                x = ref[:, pl.ds(pl.multiple_of(at, BS), BS)]
+                mom[r, s] = dot(x, x, ((0,), (0,))).astype(BF16)
+
+    def add_near(part):
+        for k in range(1, pairs + 1):
+            to_partner(k, part).wait()
+            mine = lax.rem(chip + k, pairs) * 2 + core
+
+            @pl.loop(0, slots)
+            def _(s):
+                own[k - 1, part, s] = (
+                    (old, mom)[part][mine, s].astype(F32) + near[k - 1, part, s].astype(F32)
+                ).astype(BF16)
+
+            if k < pairs:
+                to_chip(k, part).start()
+
+    for k in range(1, pairs + 1):
+        to_partner(k, 0).start()
+    add_near(0)
+    moments()
+    for k in range(1, pairs + 1):
+        to_partner(k, 1).start()
+    add_near(1)
     for part in (0, 1):
         for k in range(1, pairs):
             to_chip(k, part).wait()
 
-        @pl.loop(*pieces[part])
+        @pl.loop(0, slots)
         def _(s):
-            total = own[pairs - 1, s].astype(F32)
+            total = own[pairs - 1, part, s].astype(F32)
             for k in range(1, pairs):
-                total = total + far[k - 1, s].astype(F32)
-            out[s] = total
-
-
-def reduce_blocks(n, slots, mom):
+                total = total + far[k - 1, part, s].astype(F32)
+            if part == 0:
+                old_out[s] = total.astype(BF16)
+            else:
+                mom_out[s] = total
+
+
+def reduce_blocks(n, left, right, acts, grads, old):
+    slots = left + right
     pairs = n // 2
     vmem = pl.BlockSpec(memory_space=pltpu.VMEM)
-    buffer = pltpu.VMEM((pairs, slots, BS, BS), BF16)
+    buffer = pltpu.VMEM((pairs, 2, slots, BS, BS), BF16)
     return pl.pallas_call(
-        functools.partial(reduce_kernel, n, slots),
-        out_shape=jax.ShapeDtypeStruct((slots, BS, BS), F32),
-        in_specs=[vmem],
-        out_specs=vmem,
-        scratch_shapes=[buffer] * 3 + [pltpu.SemaphoreType.DMA((pairs, 2))] * 4,
+        functools.partial(reduce_kernel, n, left, right),
+        out_shape=[
+            jax.ShapeDtypeStruct((slots, BS, BS), F32),
+            jax.ShapeDtypeStruct((slots, BS, BS), BF16),
+        ],
+        in_specs=[vmem] * 3,
+        out_specs=[vmem, vmem],
+        scratch_shapes=[pltpu.VMEM((n, slots, BS, BS), BF16)]
+        + [buffer] * 3
+        + [pltpu.SemaphoreType.DMA((pairs, 2))] * 4,
         compiler_params=pltpu.CompilerParams(
-            collective_id=0, has_side_effects=True, vmem_limit_bytes=40 * MIB
-        ),
-        cost_estimate=pl.CostEstimate(flops=10 * MIB, bytes_accessed=16 * MIB, transcendentals=0),
+            collective_id=0, has_side_effects=True, vmem_limit_bytes=56 * MIB
+        ),
+        cost_estimate=pl.CostEstimate(flops=4096 * MIB, bytes_accessed=16 * MIB, transcendentals=0),
         name="reduce_blocks",
-    )(mom)
-
-
-def refresh_kernel(group, tokens, at, mom_ref, *refs):
-    old_refs, (out_ref, current) = refs[:group], refs[group:]
+    )(acts, grads, old)
+
+
+def refresh_kernel(group, tokens, mom_ref, old_ref, out_ref, current):
     for s in range(group):
         moment = mom_ref[s] * (1.0 / tokens)
-        product = dot(moment.astype(BF16), old_refs[s][0], ((1,), (0,)))
+        product = dot(moment.astype(BF16), old_ref[s], ((1,), (0,)))
         current[s] = product / jnp.sqrt(jnp.sum(product * product) + 1e-06)
 
     @pl.loop(0, ORTHO_STEPS)
@@ -159,34 +187,27 @@
         out_ref[s, BS:ROWS] = jnp.broadcast_to(value, (ROWS - BS, BS)).astype(BF16)
 
 
-def refresh(mom, old, at, tokens):
+def refresh(mom, old, tokens):
     slots = mom.shape[0]
     group = 4 if slots % 4 == 0 else (2 if slots % 2 == 0 else 1)
-
-    def previous(j):
-        return pl.BlockSpec((1, BS, BS), lambda i, at: (at[i * group + j], 0, 0))
-
+    block = pl.BlockSpec((group, BS, BS), lambda i: (i, 0, 0))
     return pl.pallas_call(
         functools.partial(refresh_kernel, group, tokens),
-        grid_spec=pltpu.PrefetchScalarGridSpec(
-            num_scalar_prefetch=1,
-            grid=(slots // group,),
-            in_specs=[pl.BlockSpec((group, BS, BS), lambda i, at: (i, 0, 0))]
-            + [previous(j) for j in range(group)],
-            out_specs=pl.BlockSpec((group, ROWS, BS), lambda i, at: (i, 0, 0)),
-            scratch_shapes=[pltpu.VMEM((group, BS, BS), F32)],
-        ),
+        grid=(slots // group,),
+        in_specs=[block, block],
+        out_specs=pl.BlockSpec((group, ROWS, BS), lambda i: (i, 0, 0)),
         out_shape=jax.ShapeDtypeStruct((slots, ROWS, BS), BF16),
+        scratch_shapes=[pltpu.VMEM((group, BS, BS), F32)],
         compiler_params=pltpu.CompilerParams(vmem_limit_bytes=32 * MIB),
         cost_estimate=pl.CostEstimate(
             flops=36 * slots * BS**3, bytes_accessed=8 * MIB, transcendentals=0
         ),
         name="refresh",
-    )(at, mom, *([old] * group))
+    )(mom, old)
 
 
 def spread_kernel(
-    n, columns, left, fresh, column_blocks, right, held, up_send, up_recv, down_send, down_recv,
+    n, columns, left, cuts, fresh, column_blocks, right, held, up_send, up_recv, down_send, down_recv,
     give_send, give_recv, chip_send, chip_recv, core_send, core_recv, local_sem,
 ):
     me, here = lax.axis_index("dp"), lax.axis_index("owner")
@@ -211,56 +232,58 @@
 
     held[here] = fresh[left:]
 
-    def along(k, column, send, recv, there):
-        return pltpu.make_async_remote_copy(
-            src_ref=held.at[column],
-            dst_ref=held.at[column],
-            send_sem=send.at[k],
-            recv_sem=recv.at[k],
+    def along(k, column, piece, send, recv, there):
+        return pltpu.make_async_remote_copy(
+            src_ref=held.at[column, cuts[piece]],
+            dst_ref=held.at[column, cuts[piece]],
+            send_sem=send.at[k, piece],
+            recv_sem=recv.at[k, piece],
             device_id={"owner": there},
         )
 
     def clamp(column):
         return jnp.clip(column, 0, columns - 1)
 
-    def up(k, column):
-        return along(k, clamp(column), up_send, up_recv, above)
-
-    def down(k, column):
-        return along(k, clamp(column), down_send, down_recv, below)
-
-    def give(column, target):
-        return pltpu.make_async_remote_copy(
-            src_ref=held.at[column],
-            dst_ref=right.at[me],
-            send_sem=give_send.at[target],
-            recv_sem=give_recv.at[me],
+    def up(k, column, piece):
+        return along(k, clamp(column), piece, up_send, up_recv, above)
+
+    def down(k, column, piece):
+        return along(k, clamp(column), piece, down_send, down_recv, below)
+
+    def give(column, target, piece):
+        return pltpu.make_async_remote_copy(
+            src_ref=held.at[column, cuts[piece]],
+            dst_ref=right.at[me, cuts[piece]],
+            send_sem=give_send.at[target, piece],
+            recv_sem=give_recv.at[me, piece],
             device_id={"dp": target},
         )
 
-    def taken(source):
-        return pltpu.make_async_remote_copy(
-            src_ref=held.at[0],
-            dst_ref=right.at[source],
-            send_sem=give_send.at[source],
-            recv_sem=give_recv.at[source],
+    def taken(source, piece):
+        return pltpu.make_async_remote_copy(
+            src_ref=held.at[0, cuts[piece]],
+            dst_ref=right.at[source, cuts[piece]],
+            send_sem=give_send.at[source, piece],
+            recv_sem=give_recv.at[source, piece],
             device_id={"dp": source},
         )
 
-    def keep(column):
-        return pltpu.make_async_copy(held.at[column], right.at[me], local_sem.at[0])
-
-    def share(column):
+    def keep(column, piece):
+        return pltpu.make_async_copy(
+            held.at[column, cuts[piece]], right.at[me, cuts[piece]], local_sem.at[piece]
+        )
+
+    def share(column, piece):
         for h in range(per):
             target = column * per + h
 
             @pl.when(target != me)
             def _():
-                give(column, target).start()
+                give(column, target, piece).start()
 
             @pl.when(target == me)
             def _():
-                keep(column).start()
+                keep(column, piece).start()
 
     pairs = n // 2
     chip, core = me // 2, lax.rem(me, 2)
@@ -287,69 +310,86 @@
             device_id={"dp": partner},
         )
 
-    mine = pltpu.make_async_copy(fresh, column_blocks.at[me], local_sem.at[1])
+    mine = pltpu.make_async_copy(fresh, column_blocks.at[me], local_sem.at[len(cuts)])
+    for piece in range(len(cuts)):
+
+        @pl.when(has_above)
+        def _():
+            up(0, here, piece).start()
+
+        @pl.when(has_below)
+        def _():
+            down(0, here, piece).start()
+
+    for piece in range(len(cuts)):
+        share(here, piece)
+    mine.start()
+    for j in range(1, pairs):
+        to_chip(j).start()
+    to_partner(0).start()
+
     for k in range(columns - 1):
-        sends_up = has_above & (here - k >= 0)
-        sends_down = has_below & (here + k <= columns - 1)
-
-        @pl.when(sends_up)
-        def _():
-            up(k, here - k).start()
-
-        @pl.when(sends_down)
-        def _():
-            down(k, here + k).start()
-
-        if k == 0:
-            share(here)
-            mine.start()
-            for j in range(1, pairs):
-                to_chip(j).start()
-            to_partner(0).start()
-
         if k == 1:
             for j in range(1, pairs):
                 to_chip(j).wait_recv()
                 to_partner(j).start()
-
-        @pl.when(here - 1 - k >= 0)
-        def _():
-            up(k, here - 1 - k).wait_recv()
-            share(clamp(here - 1 - k))
-
-        @pl.when(here + 1 + k <= columns - 1)
-        def _():
-            down(k, here + 1 + k).wait_recv()
-            share(clamp(here + 1 + k))
+        for piece in range(len(cuts)):
+
+            @pl.when(here - 1 - k >= 0)
+            def _():
+                up(k, here - 1 - k, piece).wait_recv()
+                if k + 1 < columns - 1:
+
+                    @pl.when(has_above)
+                    def _():
+                        up(k + 1, here - 1 - k, piece).start()
+
+                share(clamp(here - 1 - k), piece)
+
+            @pl.when(here + 1 + k <= columns - 1)
+            def _():
+                down(k, here + 1 + k, piece).wait_recv()
+                if k + 1 < columns - 1:
+
+                    @pl.when(has_below)
+                    def _():
+                        down(k + 1, here + 1 + k, piece).start()
+
+                share(clamp(here + 1 + k), piece)
 
     for k in range(columns - 1):
-
-        @pl.when(has_above & (here - k >= 0))
-        def _():
-            up(k, here - k).wait_send()
-
-        @pl.when(has_below & (here + k <= columns - 1))
-        def _():
-            down(k, here + k).wait_send()
+        for piece in range(len(cuts)):
+
+            @pl.when(has_above & (here - k >= 0))
+            def _():
+                up(k, here - k, piece).wait_send()
+
+            @pl.when(has_below & (here + k <= columns - 1))
+            def _():
+                down(k, here + k, piece).wait_send()
 
     mine.wait()
-    keep(here).wait()
     for k in range(pairs):
         to_partner(k).wait()
         if k > 0:
             to_chip(k).wait_send()
-    for k in range(1, n):
-        other = lax.rem(me + k, n)
-        taken(other).wait_send()
-        taken(other).wait_recv()
+    for piece in range(len(cuts)):
+        keep(here, piece).wait()
+        for k in range(1, n):
+            other = lax.rem(me + k, n)
+            taken(other, piece).wait_send()
+            taken(other, piece).wait_recv()
 
 
 def spread(n, columns, left, fresh):
     slots = fresh.shape[0]
     dma = pltpu.SemaphoreType.DMA
+    some = slots - left
+    pieces = 3 if some % 3 == 0 else 1
+    cuts = [pl.ds(i * (some // pieces), some // pieces) for i in range(pieces)]
     vmem = pl.BlockSpec(memory_space=pltpu.VMEM)
     return pl.pallas_call(
-        functools.partial(spread_kernel, n, columns, left),
+        functools.partial(spread_kernel, n, columns, left, cuts),
         out_shape=[
             jax.ShapeDtypeStruct((n, slots, ROWS, BS), BF16),
             jax.ShapeDtypeStruct((n, slots - left, ROWS, BS), BF16),
@@ -357,11 +397,11 @@
         in_specs=[vmem],
         out_specs=[vmem, vmem],
         scratch_shapes=[pltpu.VMEM((columns, slots - left, ROWS, BS), BF16)]
-        + [dma((columns - 1,))] * 4
-        + [dma((n,))] * 2
+        + [dma((columns - 1, pieces))] * 4
+        + [dma((n, pieces))] * 2
         + [dma((max(1, n // 2 - 1),))] * 2
         + [dma((n // 2,))] * 2
-        + [dma((2,))],
+        + [dma((pieces + 1,))],
         compiler_params=pltpu.CompilerParams(
             collective_id=1, has_side_effects=True, vmem_limit_bytes=56 * MIB
         ),
@@ -453,12 +493,14 @@
     as_int = functools.partial(jnp.array, dtype=jnp.int32)
     places = as_int([left_index(a) for a in range(blocks_a)]
                     + [g // right * slots + left + g % right for g in range(blocks_g)])
-    here = places[None, :] == (me * slots + jnp.arange(slots, dtype=jnp.int32))[:, None]
-    old_at = jnp.sum(jnp.where(here, (owners * cap + ranks)[None, :], 0), axis=1).astype(jnp.int32)
-
-    old = lax.all_gather(old_bases[0, 0], "dp", axis=0, tiled=True)
-    mom = reduce_blocks(n, slots, moments(n, left, right, acts, out_grads))
-    fresh = refresh(mom, old, old_at, tokens)
+    hit_at = places[None, :] == jnp.arange(n * slots, dtype=jnp.int32)[:, None]
+    hit_at = hit_at & (owners == me)[None, :]
+    old_at = jnp.sum(jnp.where(hit_at, ranks[None, :], 0), axis=1).astype(jnp.int32)
+    held = jnp.sum(jnp.where(hit_at, 1, 0), axis=1).astype(jnp.int32)
+
+    old = arrange(old_bases[0, 0], old_at, held).reshape(n, slots, BS, BS)
+    mom, old = reduce_blocks(n, left, right, acts, out_grads, old)
+    fresh = refresh(mom, old, tokens)
     blocks, rights = spread(n, columns, left, fresh)
     blocks = blocks.reshape(n * slots, ROWS, BS)
 

time: 243 us -> 210 us (0.86)
  waiting for transfers between devices: 21.8 us -> 0 us
  between operations: 14.2 us -> 0.74 us
    all_gather x1 -> x0, waiting for transfers between devices: 21.1 us -> none  [shards(): old = lax.all_gather(old_bases[0, 0], 'dp', axis=0, tiled=True)]
    unnamed x12 -> x14, local copies, waits for them, and re-layouts: 8.21 us -> 9.34 us
  transfers between devices with their start and end apart: 1 -> 0, of which waited for: 1 -> 0; matrix products, arithmetic and copies ran while one was open for 1% -> 0% of each run, Pallas kernels for 25% -> 0%
where the time goes in v3:
time: 210 us; the launch traced here: 208 us
  Pallas kernels  191 us (91%)
  local copies, waits for them, and re-layouts  12.7 us (6%)
  other arithmetic  2.61 us (1%)
    pallas_call x1, Pallas kernels, spread(): pl.pallas_call(functools.partial(spread_kernel, n, columns, left, cuts),...  85.8 us
    pallas_call x1, Pallas kernels, reduce_blocks(): pl.pallas_call(functools.partial(reduce_kernel, n, left, right), out_shap...  60.6 us
    pallas_call x1, Pallas kernels, precondition(): pl.pallas_call(functools.partial(precondition_kernel, rows), grid_spec=pl...  32.7 us
    pallas_call x1, Pallas kernels, refresh(): pl.pallas_call(functools.partial(refresh_kernel, group, tokens), grid=(sl...  11.1 us
    unnamed x14, local copies, waits for them, and re-layouts  9.34 us

profile of v3, /device:TPU:0, one launch (start us, length us, event | category | flops | bytes accessed | tf_op | source)
XLA Modules:
  0.0 208.2 jit_solution(10807708479605930946)
XLA Ops:
  0.6 0.7 broadcast_compare_fusion
  1.3 0.8 select_reduce_fusion.2
  2.1 0.8 select_reduce_fusion
  2.9 0.0 copy-start
  2.9 1.6 copy-done
  4.5 1.2 arrange.1
  5.7 0.0 copy-start.1
  5.7 2.0 copy-done.1
  7.7 60.6 %reduce_blocks.1 = (f32[8,256,256]{2,1,0:T(8,128)}, bf16[8,256,256]{2,1,0:T(8,128)(2,1)}) custom-call(bf16[1024,1536]{1,0:T(8,128)(2,1)} %acts.1, bf16[1024,6144]{1,0:T(8,128)(2,1)} %grads.1, bf16[4,8,256,256]{3,2,1,0:T(8,128)(2,1)} %bitcast.34), custom_call_target="tpu_custom_call" | custom-call | flops 4294967296 | bytes 16777216 | tf_op jit(solution)/shard_map/reduce_blocks/pallas_call | solution.py:145
  68.3 0.0 copy-start.4
  68.3 1.6 copy-done.4
  69.9 0.0 copy-start.5
  69.9 1.2 copy-done.5
  71.1 11.1 %refresh.1.fresh = bf16[8,272,256]{2,1,0:T(8,128)(2,1)S(1)} custom-call(f32[8,256,256]{2,1,0:T(8,128)S(1)} %copy-done.4, bf16[8,256,256]{2,1,0:T(8,128)(2,1)S(1)} %copy-done.5), custom_call_target="tpu_custom_call" | custom-call | flops 4831838208 | bytes 8388608 | tf_op jit(solution)/shard_map/refresh/pallas_call | solution.py:194
  82.2 0.0 copy-start.2
  82.2 1.0 copy-done.2
  83.2 0.0 copy-start.6
  83.2 85.8 %spread.1 = (bf16[4,8,272,256]{3,2,1,0:T(8,128)(2,1)}, bf16[4,6,272,256]{3,2,1,0:T(8,128)(2,1)}) custom-call(bf16[8,272,256]{2,1,0:T(8,128)(2,1)} %copy-done.2), custom_call_target="tpu_custom_call" | custom-call | bytes 16777216 | tf_op jit(solution)/shard_map/spread/pallas_call | solution.py:391
  168.9 0.7 slice_bitcast_fusion
  169.7 0.3 broadcast_in_dim.69.la_ref
  169.9 1.2 fusion.12
  171.1 0.1 fusion.11
  171.2 0.3 copy.11.turned_left_ref
  171.5 0.1 fusion.6
  171.6 0.0 copy-done.6
  171.7 0.1 select_reduce_fusion.3.place
  171.8 0.0 copy-start.3
  171.8 1.9 copy-done.3
  173.7 32.7 %precondition.1 = (bf16[1536,6144]{1,0:T(8,128)(2,1)}, bf16[16,256,256]{2,1,0:T(8,128)(2,1)}) custom-call(s32[16]{0:T(128)S(1)} %select_reduce_fusion.3.place, s32[16]{0:T(128)S(1)} %convert_element_type.14.used, bf16[1536,6144]{1,0:T(8,128)(2,1)} %grad_ref.1, bf16[6,256,256]{2,1,0:T(8,128)(2,1)S(1)} %get-tuple-element.27.left_ref, ...), custom_call_target="tpu_custom_call" | custom-call | flops 19327352832 | bytes 46137344 | tf_op jit(solution)/shard_map/precondition/pallas_call | solution.py:445
  206.5 0.9 slice.67
  207.4 0.8 fusion
  (2 shorter events, 0.0 us)
Async XLA Ops:
  2.9 1.6 copy-start
  5.7 2.0 copy-start.1
  68.3 1.6 copy-start.4
  69.9 1.2 copy-start.5
  82.2 1.0 copy-start.2
  83.2 88.5 %copy-start.6 = (s32[30]{0:T(128)S(1)}, s32[30]{0:T(128)}, u32[]{:S(2)}) copy-start(s32[30]{0:T(128)} %constant.13.clone) | copy-start | bytes 364
  171.8 1.9 copy-start.3

commit v4 on v3

--- a/solution.py
+++ b/solution.py
@@ -189,7 +189,7 @@
 
 def refresh(mom, old, tokens):
     slots = mom.shape[0]
-    group = 4 if slots % 4 == 0 else (2 if slots % 2 == 0 else 1)
+    group = 8 if slots % 8 == 0 else (2 if slots % 2 == 0 else 1)
     block = pl.BlockSpec((group, BS, BS), lambda i: (i, 0, 0))
     return pl.pallas_call(
         functools.partial(refresh_kernel, group, tokens),
@@ -421,9 +421,12 @@
         for a in range(rows)
     ]
     rotated = [dot(turned[a], basis, ((1,), (0,))) for a in range(rows)]
-    scaled = [
-        (rotated[a] / (la_ref[a][:, 0:1] * lg + DAMPING)).astype(BF16) for a in range(rows)
-    ]
+    scaled = []
+    for a in range(rows):
+        divisor = la_ref[a][:, 0:1] * lg + DAMPING
+        inverse = pl.reciprocal(divisor, approx=True)
+        inverse = inverse * (2.0 - divisor * inverse)
+        scaled.append((rotated[a] * inverse).astype(BF16))
     returned = [dot(scaled[a], basis, ((1,), (1,))).astype(BF16) for a in range(rows)]
     for a in range(rows):
         out_ref[a * BS : (a + 1) * BS] = dot(left_ref[a], returned[a], ((1,), (0,))).astype(BF16)

time: 210 us -> 210 us (level)
    pallas_call x1, Pallas kernels: 11.1 us -> 7.82 us  [refresh(): pl.pallas_call(functools.partial(refresh_kernel, group, tokens), grid=(sl...]
    pallas_call x1, Pallas kernels: 32.7 us -> 35.9 us  [precondition(): pl.pallas_call(functools.partial(precondition_kernel, rows), grid_spec=pl...]
where the time goes in v4:
time: 210 us; the launch traced here: 208 us
  Pallas kernels  191 us (91%)
  local copies, waits for them, and re-layouts  12.7 us (6%)
  other arithmetic  2.61 us (1%)
    pallas_call x1, Pallas kernels, spread(): pl.pallas_call(functools.partial(spread_kernel, n, columns, left, cuts),...  85.8 us
    pallas_call x1, Pallas kernels, reduce_blocks(): pl.pallas_call(functools.partial(reduce_kernel, n, left, right), out_shap...  60.6 us
    pallas_call x1, Pallas kernels, precondition(): pl.pallas_call(functools.partial(precondition_kernel, rows), grid_spec=pl...  35.9 us
    unnamed x14, local copies, waits for them, and re-layouts  9.34 us
    pallas_call x1, Pallas kernels, refresh(): pl.pallas_call(functools.partial(refresh_kernel, group, tokens), grid=(sl...  7.82 us

profile of v4, /device:TPU:0, one launch (start us, length us, event | category | flops | bytes accessed | tf_op | source)
XLA Modules:
  0.0 208.1 jit_solution(15315328542965819506)
XLA Ops:
  0.6 0.7 broadcast_compare_fusion
  1.3 0.8 select_reduce_fusion.2
  2.1 0.8 select_reduce_fusion
  2.9 0.0 copy-start
  2.9 1.6 copy-done
  4.5 1.2 arrange.1
  5.7 0.0 copy-start.1
  5.7 2.0 copy-done.1
  7.7 60.6 %reduce_blocks.1 = (f32[8,256,256]{2,1,0:T(8,128)}, bf16[8,256,256]{2,1,0:T(8,128)(2,1)}) custom-call(bf16[1024,1536]{1,0:T(8,128)(2,1)} %acts.1, bf16[1024,6144]{1,0:T(8,128)(2,1)} %grads.1, bf16[4,8,256,256]{3,2,1,0:T(8,128)(2,1)} %bitcast.34), custom_call_target="tpu_custom_call" | custom-call | flops 4294967296 | bytes 16777216 | tf_op jit(solution)/shard_map/reduce_blocks/pallas_call | solution.py:145
  68.3 0.0 copy-start.4
  68.3 1.6 copy-done.4
  69.9 0.0 copy-start.5
  69.9 1.2 copy-done.5
  71.1 7.8 %refresh.1.fresh = bf16[8,272,256]{2,1,0:T(8,128)(2,1)S(1)} custom-call(f32[8,256,256]{2,1,0:T(8,128)S(1)} %copy-done.4, bf16[8,256,256]{2,1,0:T(8,128)(2,1)S(1)} %copy-done.5), custom_call_target="tpu_custom_call" | custom-call | flops 4831838208 | bytes 8388608 | tf_op jit(solution)/shard_map/refresh/pallas_call | solution.py:194
  78.9 0.0 copy-start.2
  78.9 1.0 copy-done.2
  79.9 0.0 copy-start.6
  79.9 85.8 %spread.1 = (bf16[4,8,272,256]{3,2,1,0:T(8,128)(2,1)}, bf16[4,6,272,256]{3,2,1,0:T(8,128)(2,1)}) custom-call(bf16[8,272,256]{2,1,0:T(8,128)(2,1)} %copy-done.2), custom_call_target="tpu_custom_call" | custom-call | bytes 16777216 | tf_op jit(solution)/shard_map/spread/pallas_call | solution.py:391
  165.7 0.7 slice_bitcast_fusion
  166.4 0.3 broadcast_in_dim.69.la_ref
  166.7 1.2 fusion.12
  167.9 0.1 fusion.11
  168.0 0.3 copy.11.turned_left_ref
  168.3 0.1 fusion.6
  168.4 0.0 copy-done.6
  168.4 0.1 select_reduce_fusion.3.place
  168.5 0.0 copy-start.3
  168.5 1.9 copy-done.3
  170.5 35.9 %precondition.1 = (bf16[1536,6144]{1,0:T(8,128)(2,1)}, bf16[16,256,256]{2,1,0:T(8,128)(2,1)}) custom-call(s32[16]{0:T(128)S(1)} %select_reduce_fusion.3.place, s32[16]{0:T(128)S(1)} %convert_element_type.14.used, bf16[1536,6144]{1,0:T(8,128)(2,1)} %grad_ref.1, bf16[6,256,256]{2,1,0:T(8,128)(2,1)S(1)} %get-tuple-element.27.left_ref, ...), custom_call_target="tpu_custom_call" | custom-call | flops 19327352832 | bytes 46137344 | tf_op jit(solution)/shard_map/precondition/pallas_call | solution.py:448
  206.4 0.9 slice.67
  207.3 0.8 fusion
  (2 shorter events, 0.0 us)
Async XLA Ops:
  2.9 1.6 copy-start
  5.7 2.0 copy-start.1
  68.3 1.6 copy-start.4
  69.9 1.2 copy-start.5
  78.9 1.0 copy-start.2
  79.9 88.5 %copy-start.6 = (s32[30]{0:T(128)S(1)}, s32[30]{0:T(128)}, u32[]{:S(2)}) copy-start(s32[30]{0:T(128)} %constant.13.clone) | copy-start | bytes 364
  168.5 1.9 copy-start.3
